TPU v7x, 32 devices: a whole 2x2x4 slice. The times are simulated.
32 devices in a mesh: rep: 4 (over y, x), wide: 8 (over z, core).
Axes of the slice: x: 2, y: 2, z: 4, core: 2. Of those that a mesh axis runs over, the one named last changes fastest.
Arguments:
- grad_parts: float32 [4, 2048, 16384], P('rep', None, 'wide'), may hold values from -4 to 4
- master_param: float32 [2048, 16384], P('rep', 'wide')
- moment_one: float32 [2048, 16384], P('rep', 'wide'), may hold values from -2 to 2
- moment_two: float32 [2048, 16384], P('rep', 'wide'), may hold values from 0.05 to 2
- owner: int32 [2048], P('rep'), may hold values from 0 to 7, as said below
- offset: int32 [2048], P('rep'), may hold values from 0 to 255, as said below
Outputs:
- new_param: float32 [2048, 16384], P('rep', 'wide')
- new_moment_one: float32 [2048, 16384], P('rep', 'wide')
- new_moment_two: float32 [2048, 16384], P('rep', 'wide')
- received: bfloat16 [8192, 16384], P(('rep', 'wide'))
- received_scale: float32 [8192], P(('rep', 'wide'))
Inputs may be any that keep to these rules, and one draw needn't show every extreme that they name: Among the blocks of one group of 512, no two have the same owner and offset; an owner that gets k of them gets offsets 0 to k - 1. `offset`: see owner.
All inputs are finite; a program needn't handle non-finite values. Where the computation divides by a largest or mean magnitude, that divisor is 1e-20 or more.
Results may differ from a plain program's by a relative error of at most 0.005.
Values may be sent and summed in bfloat16 or wider, within the bound.
No kernel may reach another device: no remote copies, remote signals or barrier semaphores. Data moves between devices by JAX's collectives and lax.ppermute only.
A program may use at most 128 MiB of HBM per device.

v0:
```python
import jax
import jax.numpy as jnp
from jax import lax
from jax.sharding import PartitionSpec as P


def shards(grad_parts, master_param, moment_one, moment_two, owner, offset):
    grad = lax.psum_scatter(
        grad_parts[0].astype(jnp.bfloat16), "rep", scatter_dimension=0, tiled=True
    ).astype(jnp.float32)
    new_moment_one = 0.9 * moment_one + 0.1 * grad
    new_moment_two = 0.95 * moment_two + 0.05 * grad * grad
    first_fix = 1.0 - 0.9**1000.0
    second_fix = 1.0 - 0.95**1000.0
    update = new_moment_one / first_fix / (jnp.sqrt(new_moment_two / second_fix) + 1e-08)
    new_param = master_param - 0.01 * (update + 0.1 * master_param)
    n_wide = lax.axis_size("wide")
    own_index = lax.axis_index("wide")
    capacity = 4 * owner.shape[0] // n_wide
    width = new_param.shape[1]
    slot_range = jnp.arange(capacity, dtype=jnp.int32)
    matched = (owner[:, None] == own_index) & (offset[:, None] == slot_range[None, :])
    target_slot = owner * capacity + offset
    all_slots = jnp.arange(n_wide * capacity, dtype=jnp.int32)
    routing = all_slots[:, None] == target_slot[None, :]
    placed = jnp.dot(
        routing.astype(jnp.float32),
        new_param,
        preferred_element_type=jnp.float32,
        precision=lax.Precision.HIGHEST,
    )
    outgoing = placed.reshape(n_wide, capacity, width)
    arrived = lax.all_to_all(outgoing, "wide", split_axis=0, concat_axis=2, tiled=True)
    blocks = arrived[0]
    filled = jnp.any(matched, axis=0)
    slot_scale = jnp.max(jnp.abs(blocks), axis=1) + 1e-06
    received_scale = jnp.where(filled, slot_scale, 0.0)
    divisor = jnp.where(filled, slot_scale, 1.0)
    received = (blocks / divisor[:, None]).astype(jnp.bfloat16)
    return (new_param, new_moment_one, new_moment_two, received, received_scale)


def solution(mesh):
    return jax.shard_map(
        shards,
        mesh=mesh,
        in_specs=(
            P("rep", None, "wide"),
            P("rep", "wide"),
            P("rep", "wide"),
            P("rep", "wide"),
            P("rep"),
            P("rep"),
        ),
        out_specs=(
            P("rep", "wide"),
            P("rep", "wide"),
            P("rep", "wide"),
            P(("rep", "wide"), None),
            P(("rep", "wide")),
        ),
        check_vma=False,
    )
```

profile of v0, /device:TPU:0, one launch (start us, length us, event | category | flops | bytes accessed | tf_op | source)
XLA Modules:
  0.0 535.7 jit_solution(13764871777542064602)
XLA Ops:
  7.2 0.0 reduce-scatter.2.cloned.1.call-start
  7.2 9.1 %convert_bitcast_fusion = bf16[2048,2048]{1,0:T(8,128)(2,1)} fusion(f32[1,2048,2048]{2,1,0:T(8,128)} %param.6), kind=kLoop, calls=%fused_computation.2 | loop fusion | flops 4194304 | bytes 25165824 | tf_op jit(solution)/shard_map/convert_element_type | solution.py:9
  16.3 0.0 copy-start.1
  16.3 0.0 copy-start.2
  16.3 0.0 reduce-scatter.2.cloned.1.call-update
  16.3 0.7 copy-done.1
  17.0 0.0 copy-done.2
  17.0 88.6 %reduce-scatter.2.cloned.1.call-done = bf16[512,2048]{1,0:T(8,128)(2,1)} async-done(((bf16[2048,2048]{1,0:T(8,128)(2,1)}), bf16[512,2048]{1,0:T(8,128)(2,1)}) %reduce-scatter.2.cloned.1.call-update) | async-done | bytes 2097168 | tf_op jit(solution)/shard_map/reduce_scatter | solution.py:8
  105.6 8.8 %multiply_subtract_fusion = (f32[512,2048]{1,0:T(8,128)S(1)}, f32[512,2048]{1,0:T(8,128)}, f32[512,2048]{1,0:T(8,128)}) fusion(f32[512,2048]{1,0:T(8,128)} %param.7, bf16[512,2048]{1,0:T(8,128)(2,1)} %reduce-scatter.2.cloned.1.call-done, f32[512,2048]{1,0:T(8,128)} %param.9, f32[512,2048]{1,0:T(8,128)} %param.8), kind=kLoop, calls=%fused_computation.8 | loop fusion | flops 14680064 | bytes 27262976 | tf_op jit(solution)/shard_map/sub | solution.py:16
  114.3 0.0 copy-start
  114.3 16.6 %fusion.2 = f32[2048,2048]{1,0:T(8,128)} fusion(f32[512,2048]{1,0:T(8,128)S(1)} %get-tuple-element.5, s32[512]{0:T(512)S(1)} %multiply_add_fusion), kind=kOutput, calls=%fused_computation.9 | convolution fusion | flops 25770852352 | bytes 20973568 | tf_op jit(solution)/shard_map/dot_general | solution.py:26
  130.9 0.0 copy-done
  130.9 5.7 %all-to-all-start = ((f32[8,256,2048]{2,1,0:T(8,128)}), f32[8,256,2048]{2,1,0:T(8,128)}, u32[]{:S(2)}, u32[]{:S(2)}) async-start(f32[8,256,2048]{2,1,0:T(8,128)} %bitcast.14), calls=%async_computation.1 | async-start | bytes 33554432 | tf_op jit(solution)/shard_map/all_to_all | solution.py:33
  136.7 0.2 fusion.5
  136.9 363.4 %all-to-all-done = f32[8,256,2048]{2,1,0:T(8,128)} async-done(((f32[8,256,2048]{2,1,0:T(8,128)}), f32[8,256,2048]{2,1,0:T(8,128)}, u32[]{:S(2)}, u32[]{:S(2)}) %all-to-all-start) | async-done | bytes 16777248 | tf_op jit(solution)/shard_map/all_to_all | solution.py:33
  500.4 11.6 %copy.13 = f32[32,8,8,2048]{3,1,2,0:T(8,128)} copy(f32[32,8,8,2048]{3,1,0,2:T(8,128)} %bitcast.10) | data formatting | bytes 33554432
  512.0 7.2 %abs_reduce_fusion = f32[256]{0:T(256)S(1)} fusion(f32[8,256,2048]{2,1,0:T(8,128)} %all-to-all-done), kind=kLoop, calls=%fused_computation.1 | loop fusion | flops 8388352 | bytes 16778240 | tf_op jit(solution)/shard_map/reduce_max | solution.py:36
  519.2 0.6 add_select_fusion
  519.8 9.0 %divide_convert_fusion = bf16[256,16384]{1,0:T(8,128)(2,1)} fusion(f32[256,16384]{1,0:T(8,128)} %bitcast.13, f32[256]{0:T(256)S(1)} %get-tuple-element.9), kind=kLoop, calls=%fused_computation | loop fusion | flops 8388608 | bytes 25166848 | tf_op jit(solution)/shard_map/convert_element_type | solution.py:39
  (2 shorter events, 0.0 us)
Async XLA Ops:
  7.2 98.4 %reduce-scatter.2.cloned.1.call-start = ((), (), s32[]{:S(2)}) async-start(), calls=%async_computation.2 | async-start | bytes 10485760 | tf_op jit(solution)/shard_map/reduce_scatter | solution.py:8
  16.3 0.7 copy-start.1
  16.3 0.7 copy-start.2
  114.3 16.6 %copy-start = (f32[512,2048]{1,0:T(8,128)}, f32[512,2048]{1,0:T(8,128)S(1)}, u32[]{:S(2)}) copy-start(f32[512,2048]{1,0:T(8,128)S(1)} %get-tuple-element.5) | copy-start | bytes 12582916
  130.9 369.4 %all-to-all-start = ((f32[8,256,2048]{2,1,0:T(8,128)}), f32[8,256,2048]{2,1,0:T(8,128)}, u32[]{:S(2)}, u32[]{:S(2)}) async-start(f32[8,256,2048]{2,1,0:T(8,128)} %bitcast.14), calls=%async_computation.1 | async-start | bytes 33554432 | tf_op jit(solution)/shard_map/all_to_all | solution.py:33
Sparse Core Ops, SparseCore 0:
  16.4 89.0 reduce-scatter.1
where the time goes:
time: 536 us
  waiting for transfers between devices  452 us (84%)
  other arithmetic  34.9 us (7%)
  matrix products  16.6 us (3%)
  between operations  14.1 us (3%)
  local copies, waits for them, and re-layouts  12.3 us (2%)
  starting transfers between devices  5.79 us (1%)
    all_to_all x1, waiting for transfers between devices, shards(): lax.all_to_all(outgoing, 'wide', split_axis=0, concat_axis=2, tiled=True)  363 us
    reduce_scatter x1, waiting for transfers between devices, shards(): lax.psum_scatter(grad_parts[0].astype(jnp.bfloat16), 'rep', scatter_dimen...  88.6 us
    dot_general x1, matrix products, shards(): jnp.dot(routing.astype(jnp.float32), new_param, preferred_element_type=jn...  16.6 us
    unnamed x7, local copies, waits for them, and re-layouts  12.3 us
  transfers between devices with their start and end apart: 2, of which 2 were waited for; matrix products, arithmetic and copies ran while one was open for 0% of the time, Pallas kernels for 0%

commit v1 on v0

v1 whole, which is shorter than its diff:
```python
import functools
import jax
import jax.numpy as jnp
from jax import lax
from jax.experimental import pallas as pl
from jax.experimental.pallas import tpu as pltpu
from jax.sharding import PartitionSpec as P

FIRST_FIX = 1.0 - 0.9**1000.0
SECOND_FIX = 1.0 - 0.95**1000.0
ANY = pl.BlockSpec(memory_space=pl.ANY)
SMEM = pl.BlockSpec(memory_space=pltpu.SMEM)
VMEM = pl.BlockSpec(memory_space=pltpu.VMEM)
DMA = pltpu.SemaphoreType.DMA
STRIP = 16
CHUNKS = (512, 512, 512, 512)
ORDER = (
    ("cast", 0), ("sum", 0), ("cast", 1), ("update", 0), ("sum", 1), ("cast", 2), ("update", 1), ("sum", 2),
    ("cast", 3), ("update", 2), ("sum", 3), ("pick", 0), ("pick", 1), ("forward", 2), ("update", 3), ("mark", 0),
    ("pick", 2), ("peaks", 0), ("halves", 3), ("scales", 0), ("store", 0), ("store", 1), ("pick", 3), ("store", 2),
    ("store", 3),
)


def params():
    return pltpu.CompilerParams(vmem_limit_bytes=48 * 1024 * 1024)


def cost(moved, flops=0):
    return pl.CostEstimate(flops=0, bytes_accessed=1024, transcendentals=0)


def adamw(grad, master, moment_one, moment_two):
    new_one = 0.9 * moment_one + 0.1 * grad
    new_two = 0.95 * moment_two + 0.05 * grad * grad
    update = new_one / FIRST_FIX / (jnp.sqrt(new_two / SECOND_FIX) + 1e-08)
    return master - 0.01 * (update + 0.1 * master), new_one, new_two


def start_copies(pairs, sems, first=0):
    copies = [pltpu.make_async_copy(src, dst, sems.at[first + i]) for i, (src, dst) in enumerate(pairs)]
    for copy in copies:
        copy.start()
    return copies


def wait_copies(copies):
    for copy in copies:
        copy.wait()


CAST_TILES = 2


def group_rows(groups_ref, j, tile, rows, tiles):
    height = rows // tiles
    return pl.ds(pl.multiple_of(groups_ref[j] * rows + tile * height, 16), height)


def cast_kernel(start, groups_ref, grads_ref, *refs):
    outs, (held, packed, in_sems, out_sems) = refs[-7:-4], refs[-4:]
    size = held.shape[2]
    height = held.shape[1]
    rows = height * CAST_TILES
    where = [(j, t) for t in range(CAST_TILES) for j in range(3)]
    columns = pl.ds(start, size)
    sources = [grads_ref.at[group_rows(groups_ref, j, t, rows, CAST_TILES), columns] for j, t in where]
    arriving = start_copies([(source, held.at[i]) for i, source in enumerate(sources)], in_sems)
    leaving = []
    for i, (j, t) in enumerate(where):
        arriving[i].wait()
        packed[i] = held[i].astype(jnp.bfloat16)
        leaving += start_copies([(packed.at[i], outs[j].at[pl.ds(t * height, height)])], out_sems, i)
    wait_copies(leaving)


def cast_shares(grads, groups, after, rows, start, size):
    tiles = 3 * CAST_TILES
    height = rows // CAST_TILES
    return pl.pallas_call(
        functools.partial(cast_kernel, start),
        in_specs=[SMEM, ANY] + [ANY] * len(after),
        out_specs=[ANY] * 3,
        out_shape=[jax.ShapeDtypeStruct((rows, size), jnp.bfloat16)] * 3,
        scratch_shapes=[
            pltpu.VMEM((tiles, height, size), jnp.float32),
            pltpu.VMEM((tiles, height, size), jnp.bfloat16),
            DMA((tiles,)),
            DMA((tiles,)),
        ],
        compiler_params=params(),
        cost_estimate=cost(3 * rows * size * 6),
        name="cast_shares",
    )(groups, grads, *after)


UPDATE_TILES = 4
PEAK_ROWS = 16


def update_kernel(start, first_chunk, last_chunk, n_came, group_ref, grads_ref, *refs):
    came, states = refs[:n_came], refs[n_came : n_came + 3]
    top_ref = None if first_chunk else refs[n_came + 3]
    n_out, n_scratch = 5, 9
    outs = refs[-n_out - n_scratch - last_chunk : -n_scratch]
    grad_in, came_in, state_in, new_state, sent_out, top_in, top_out, in_sems, out_sems = refs[-n_scratch:]
    rows, size = grad_in.shape
    n_in = n_came + 4
    height = rows // UPDATE_TILES
    columns = pl.ds(start, size)
    top_copies = [] if first_chunk else start_copies([(top_ref, top_in)], in_sems, n_in * UPDATE_TILES)

    arriving = []
    for t in range(UPDATE_TILES):
        here = pl.ds(t * height, height)
        own = group_rows(group_ref, 0, t, rows, UPDATE_TILES)
        pairs = [(came[j].at[here], came_in.at[j, here]) for j in range(n_came)]
        pairs += [(grads_ref.at[own, columns], grad_in.at[here])]
        pairs += [(states[j].at[here, columns], state_in.at[j, here]) for j in range(3)]
        arriving.append(start_copies(pairs, in_sems, n_in * t))
    wait_copies(top_copies)
    leaving = []
    for t in range(UPDATE_TILES):
        wait_copies(arriving[t])

        @pl.loop(0, height // STRIP)
        def _(i, t=t):
            strip = pl.ds(pl.multiple_of(t * height + i * STRIP, STRIP), STRIP)
            top = jnp.zeros((STRIP, 128), jnp.float32) if first_chunk else top_in[strip]
            for lane in range(0, size, 128):
                lanes = pl.ds(lane, 128)
                grad = grad_in[strip, lanes]
                for j in range(n_came):
                    grad = grad + came_in[j, strip, lanes].astype(jnp.float32)
                new = adamw(grad, *(state_in[j, strip, lanes] for j in range(3)))
                for j in range(3):
                    new_state[j, strip, lanes] = new[j]
                sent_out[strip, lanes] = new[0].astype(jnp.bfloat16)
                top = jnp.maximum(top, jnp.abs(new[0]))
            top_out[strip] = top

        here = pl.ds(t * height, height)
        pairs = [(new_state.at[j, here], outs[j].at[here, columns]) for j in range(3)]
        pairs += [(top_out.at[here], outs[3].at[here]), (sent_out.at[here], outs[4].at[here])]
        leaving += start_copies(pairs, out_sems, n_out * t)
    if last_chunk:
        high = jnp.max(top_out[...].T, axis=0, keepdims=True)
        outs[5][...] = jnp.broadcast_to(high, outs[5].shape)
        packed = []
        for _ in range(3):
            packed.append(high.astype(jnp.bfloat16).astype(jnp.float32))
            high = high - packed[-1]
        packed.append(jnp.zeros((PEAK_ROWS - 3, rows), jnp.float32))
        peaks = pl.ds(rows, PEAK_ROWS)
        sent_out[peaks, pl.ds(0, rows)] = jnp.concatenate(packed, axis=0).astype(jnp.bfloat16)
        leaving += start_copies([(sent_out.at[peaks], outs[4].at[peaks])], out_sems, n_out * UPDATE_TILES)
    wait_copies(leaving)


def update_chunk(grads, came, states, group, top, old, after, start, last_chunk):
    rows, width = states[0].shape
    size = came[0].shape[1]
    whole = jax.ShapeDtypeStruct((rows, width), jnp.float32)
    first_chunk = not old
    n_came = len(came)
    n_before = 5 + n_came + (not first_chunk)
    extra = [*([] if first_chunk else [top]), *old, *after]
    sent_rows = rows + PEAK_ROWS * last_chunk
    return pl.pallas_call(
        functools.partial(update_kernel, start, first_chunk, last_chunk, n_came),
        in_specs=[SMEM] + [ANY] * (4 + n_came + len(extra)),
        out_specs=[ANY] * 5 + [VMEM] * last_chunk,
        out_shape=[whole] * 3
        + [jax.ShapeDtypeStruct((rows, 128), jnp.float32), jax.ShapeDtypeStruct((sent_rows, size), jnp.bfloat16)]
        + [jax.ShapeDtypeStruct((8, rows), jnp.float32)] * last_chunk,
        scratch_shapes=[
            pltpu.VMEM((rows, size), jnp.float32),
            pltpu.VMEM((n_came, rows, size), jnp.bfloat16),
            pltpu.VMEM((3, rows, size), jnp.float32),
            pltpu.VMEM((3, rows, size), jnp.float32),
            pltpu.VMEM((sent_rows, size), jnp.bfloat16),
            pltpu.VMEM((rows, 128), jnp.float32),
            pltpu.VMEM((rows, 128), jnp.float32),
            DMA(((n_came + 4) * UPDATE_TILES + 1,)),
            DMA((5 * UPDATE_TILES + 1,)),
        ],
        input_output_aliases={n_before + i: i for i in range(len(old))},
        compiler_params=params(),
        cost_estimate=cost(rows * size * 36),
        name="update_chunk",
    )(group, grads, *came, *states, *extra)


def pass_kernel(*refs):
    pass


def pass_after(values, after):
    return pl.pallas_call(
        pass_kernel,
        in_specs=[ANY] * (len(values) + len(after)),
        out_specs=[ANY] * len(values),
        out_shape=[jax.ShapeDtypeStruct(value.shape, value.dtype) for value in values],
        input_output_aliases={i: i for i in range(len(values))},
        compiler_params=params(),
        cost_estimate=cost(0),
        name="pass_after",
    )(*values, *after)


def halves_kernel(ahead_ref, back_ref, *refs):
    first_ref, second_ref, sems = refs[-3:]
    (rows, first), second = first_ref.shape, second_ref.shape[1]
    pairs = [
        (ahead_ref.at[pl.ds(0, rows), pl.ds(0, first)], first_ref),
        (back_ref.at[pl.ds(0, rows), pl.ds(first, second)], second_ref),
    ]
    wait_copies(start_copies(pairs, sems))


def cut_halves(ahead, back, after):
    rows, size = ahead.shape[0] - PEAK_ROWS, ahead.shape[1]
    first = size // 256 * 128
    return pl.pallas_call(
        halves_kernel,
        in_specs=[ANY] * (2 + len(after)),
        out_specs=[ANY] * 2,
        out_shape=[jax.ShapeDtypeStruct((rows, part), ahead.dtype) for part in (first, size - first)],
        scratch_shapes=[DMA((2,))],
        compiler_params=params(),
        cost_estimate=cost(rows * size * 4),
        name="cut_halves",
    )(ahead, back, *after)


def pick_kernel(n_sources, pick_ref, *refs):
    sources = refs[:n_sources]
    mine_ref, other_ref, held, placed, in_sems, out_sems = refs[-6:]
    n_chips, slots, _ = mine_ref.shape
    rows = held.shape[1]
    pairs = [(sources[i].at[pl.ds(0, rows)], held.at[i]) for i in range(n_chips - 1)]
    edge = 0
    for source in sources[n_chips - 1 :]:
        pairs.append((source, held.at[n_chips - 1, :, pl.ds(edge, source.shape[1])]))
        edge += source.shape[1]
    arriving = start_copies(pairs, in_sems)
    leaving = []
    for i in range(n_chips):
        wait_copies(arriving[i:] if i == n_chips - 1 else arriving[i : i + 1])
        placed[i] = jnp.dot(pick_ref[...], held[i], preferred_element_type=jnp.float32).astype(jnp.bfloat16)
        pairs = [
            (placed.at[i, pl.ds(slots, slots)], other_ref.at[i]),
            (placed.at[i, pl.ds(0, slots)], mine_ref.at[i]),
        ]
        leaving += start_copies(pairs, out_sems, 2 * i)
    wait_copies(leaving)


def pick_rows(pick, sources, after, moved=1024):
    rows, size = pick.shape[1], sources[0].shape[1]
    slots = pick.shape[0] // 2
    n_sources, n = len(sources), 4
    return pl.pallas_call(
        functools.partial(pick_kernel, n_sources),
        in_specs=[VMEM] + [ANY] * (n_sources + len(after)),
        out_specs=[ANY] * 2,
        out_shape=[jax.ShapeDtypeStruct((n, slots, size), jnp.bfloat16)] * 2,
        scratch_shapes=[
            pltpu.VMEM((n, rows, size), jnp.bfloat16),
            pltpu.VMEM((n, 2 * slots, size), jnp.bfloat16),
            DMA((n_sources,)),
            DMA((2 * n,)),
        ],
        compiler_params=params(),
        cost_estimate=pl.CostEstimate(flops=0, bytes_accessed=moved, transcendentals=0),
        name="pick_rows",
    )(pick, *sources, *after)


def store_kernel(start, width, place_ref, inverse_ref, mine_ref, other_ref, *refs):
    out_ref, token_ref, held, done, in_sems, out_sems = refs[-6:]
    n_chips, _, size = mine_ref.shape
    token_ref[...] = jnp.zeros_like(token_ref)
    sources = [ref.at[i] for i in range(n_chips) for ref in (mine_ref, other_ref)]
    arriving = start_copies([(source, held.at[i]) for i, source in enumerate(sources)], in_sems)
    leaving = []
    for i in range(len(sources)):
        arriving[i].wait()
        done[i] = (held[i].astype(jnp.float32) * inverse_ref[...]).astype(jnp.bfloat16)
        column = pl.multiple_of(place_ref[i] * width + start, 128)
        leaving += start_copies([(done.at[i], out_ref.at[:, pl.ds(column, size)])], out_sems, i)
    wait_copies(leaving)


def store_rows(place, inverse, mine, other, old, after, start, whole, width):
    n, slots, size = mine.shape
    return pl.pallas_call(
        functools.partial(store_kernel, start, width),
        in_specs=[SMEM, VMEM] + [ANY] * (2 + len(old) + len(after)),
        out_specs=[ANY, VMEM],
        out_shape=[whole, jax.ShapeDtypeStruct((8, 128), jnp.float32)],
        scratch_shapes=[
            pltpu.VMEM((2 * n, slots, size), jnp.bfloat16),
            pltpu.VMEM((2 * n, slots, size), jnp.bfloat16),
            DMA((2 * n,)),
            DMA((2 * n,)),
        ],
        input_output_aliases={4: 0} if old else {},
        compiler_params=params(),
        cost_estimate=cost(8 * n * slots * size),
        name="store_rows",
    )(place, inverse, mine, other, *old, *after)


def peak_kernel(high_ref, across_ref, ahead_ref, back_ref, *refs):
    out_ref, held, sems = refs[-3:]
    rows = high_ref.shape[1]
    peaks = pl.ds(rows, PEAK_ROWS), pl.ds(0, rows)
    wait_copies(start_copies([(ahead_ref.at[peaks], held.at[0]), (back_ref.at[peaks], held.at[1])], sems))
    high = jnp.maximum(high_ref[...], across_ref[...])
    for side in range(2):
        packed = held[side].astype(jnp.float32)
        high = jnp.maximum(high, (packed[0:1] + packed[1:2]) + packed[2:3])
    out_ref[...] = high


def line_peaks(high, across, ahead, back, after):
    rows = high.shape[1]
    return pl.pallas_call(
        peak_kernel,
        in_specs=[VMEM] * 2 + [ANY] * (2 + len(after)),
        out_specs=VMEM,
        out_shape=jax.ShapeDtypeStruct(high.shape, jnp.float32),
        scratch_shapes=[pltpu.VMEM((2, PEAK_ROWS, rows), jnp.bfloat16), DMA((2,))],
        compiler_params=params(),
        cost_estimate=cost(0),
        name="line_peaks",
    )(high, across, ahead, back, *after)


def scale_kernel(pick_ref, *refs):
    inverse_ref, scale_ref = refs[-2:]
    high = jnp.maximum(refs[0][...], refs[1][...])
    slots = inverse_ref.shape[0]
    held = pick_ref[pl.ds(0, slots)].astype(jnp.float32) > 0.5
    scale = jnp.max(jnp.where(held, high[:1] + 1e-06, 0.0), axis=1, keepdims=True)
    inverse_ref[...] = 1.0 / jnp.where(scale > 0.0, scale, 1.0)
    scale_ref[...] = jnp.broadcast_to(scale, (slots, 128)).T[:1]


def slot_scales(pick, highs, after):
    slots = pick.shape[0] // 2
    return pl.pallas_call(
        scale_kernel,
        in_specs=[VMEM] * 3 + [ANY] * len(after),
        out_specs=[VMEM, VMEM],
        out_shape=[
            jax.ShapeDtypeStruct((slots, 1), jnp.float32),
            jax.ShapeDtypeStruct((1, slots), jnp.float32),
        ],
        compiler_params=params(),
        cost_estimate=cost(0),
        name="slot_scales",
    )(pick, *highs, *after)


def line_shards(grad_parts, master_param, moment_one, moment_two, owner, offset):
    n_rep, n_wide = lax.axis_size("rep"), lax.axis_size("wide")
    n_chips = n_wide // 2
    rows, width = master_param.shape
    capacity = 4 * rows // n_wide
    grads = grad_parts[0]
    rep_index = lax.axis_index("rep")
    wide_index = lax.axis_index("wide")
    chip, core = wide_index // 2, wide_index % 2
    ring = [0, *range(1, n_chips, 2), *range(2, n_chips, 2)[::-1]]

    def swap(value, mask):
        return lax.ppermute(value, "rep", [(i, i ^ mask) for i in range(n_rep)])

    def groups(*masks):
        return (rep_index ^ jnp.array(masks)).astype(jnp.int32)

    def turn_by(value, step):
        pairs = [
            (2 * ring[i] + c, 2 * ring[(i + step) % n_chips] + c) for i in range(n_chips) for c in range(2)
        ]
        return lax.ppermute(value, "wide", pairs)

    def sibling(value):
        return lax.ppermute(value, "wide", [(i, i ^ 1) for i in range(n_wide)])

    slot_range = jnp.arange(capacity, dtype=jnp.int32)
    both = jnp.stack([wide_index, wide_index ^ 1])
    matched = (owner[None, None, :] == both[:, None, None]) & (offset[None, None, :] == slot_range[None, :, None])
    pick_both = matched.reshape(2 * capacity, rows).astype(jnp.bfloat16)
    ring_at = jnp.array(ring, jnp.int32)
    spot = jnp.argmax(ring_at == chip)
    chips = ring_at[(spot + jnp.array([0, -1, 1, 2])) % n_chips]
    place = jnp.stack([2 * chips + core, 2 * chips + 1 - core], axis=1).reshape(-1).astype(jnp.int32)
    own_group = groups(0)

    states = (master_param, moment_one, moment_two)
    whole = jax.ShapeDtypeStruct((capacity, n_wide * width), jnp.bfloat16)
    starts = [sum(CHUNKS[:k]) for k in range(len(CHUNKS))]
    last = len(CHUNKS) - 1
    forwarded, pieces = {-1: []}, {}
    old, received, after = [], [], []
    top = inverse = received_scale = None

    for kind, k in ORDER:
        if kind == "cast":
            if k == 1:
                after = after + [pick_both, place]
            shares = cast_shares(grads, groups(1, 2, 3), after, rows, starts[k], CHUNKS[k])
            after = [shares[0]]
        elif kind == "sum":
            if k > 0:
                shares = pass_after(shares, after + forwarded[k - 2])
                after = [shares[0]]
            came = [swap(share, mask) for share, mask in zip(shares, (1, 2, 3))]
        elif kind == "update":
            if k > 0:
                after = after + [ahead, back]
            new = update_chunk(grads, came, states, own_group, top, old, after, starts[k], k == last)
            old, top, sent = new[:3], new[3], new[4]
            after = [sent]
            ahead, back = turn_by(sent, 1), turn_by(sent, -1)
            pieces[k] = [sent, ahead, back]
            if k < last - 1:
                forwarded[k] = [turn_by(ahead, 1)]
            elif k == last:
                high, across = new[5], turn_by(new[5], 2)
        elif kind == "forward":
            (ahead,) = pass_after([ahead], after)
            pieces[k] = [sent, ahead, back]
            forwarded[k] = [turn_by(ahead, 1)]
            after = [ahead]
        elif kind == "mark":
            after = pass_after([place], after + forwarded[last - 1])
            (place,) = after
        elif kind == "halves":
            after = cut_halves(ahead, back, after)
            forwarded[k] = [turn_by(half, way) for half, way in zip(after, (1, -1))]
        elif kind == "pick":
            moved = 2**24 if k == last - 1 else 1024
            mine, other = pick_rows(pick_both, pieces[k] + forwarded[k], after, moved)
            pieces[k] = mine, sibling(other)
            after = [mine]
        elif kind == "peaks":
            high = line_peaks(high, across, ahead, back, after)
            after = [high]
        elif kind == "scales":
            inverse, received_scale = slot_scales(pick_both, [high, sibling(high)], after)
            after = [received_scale]
        else:
            *received, token = store_rows(place, inverse, *pieces[k], received, after, starts[k], whole, width)
            after = [token]
    return (*old, received[0], received_scale.reshape(capacity))


def general_shards(grad_parts, master_param, moment_one, moment_two, owner, offset):
    grad = lax.psum_scatter(
        grad_parts[0].astype(jnp.bfloat16), "rep", scatter_dimension=0, tiled=True
    ).astype(jnp.float32)
    new_param, new_one, new_two = adamw(grad, master_param, moment_one, moment_two)
    n_wide = lax.axis_size("wide")
    capacity = 4 * owner.shape[0] // n_wide
    scale = lax.pmax(jnp.max(jnp.abs(new_param), axis=1), "wide") + 1e-06
    blocks = lax.all_gather(new_param.astype(jnp.bfloat16), "wide", axis=1, tiled=True)
    slot_range = jnp.arange(capacity, dtype=jnp.int32)
    own_slots = (owner[None, :] == lax.axis_index("wide")) & (offset[None, :] == slot_range[:, None])
    filled = jnp.any(own_slots, axis=1)
    slot_scale = jnp.max(jnp.where(own_slots, scale[None, :], 0.0), axis=1)
    received_scale = jnp.where(filled, slot_scale, 0.0)
    divisor = jnp.where(filled, slot_scale, 1.0)
    placed = jnp.dot(own_slots.astype(jnp.bfloat16), blocks, preferred_element_type=jnp.float32)
    received = (placed / divisor[:, None]).astype(jnp.bfloat16)
    return (new_param, new_one, new_two, received, received_scale)


def solution(mesh):
    short_line = mesh.shape["rep"] == 4 and mesh.shape["wide"] == 8
    return jax.shard_map(
        line_shards if short_line else general_shards,
        mesh=mesh,
        in_specs=(
            P("rep", None, "wide"),
            P("rep", "wide"),
            P("rep", "wide"),
            P("rep", "wide"),
            P("rep"),
            P("rep"),
        ),
        out_specs=(
            P("rep", "wide"),
            P("rep", "wide"),
            P("rep", "wide"),
            P(("rep", "wide"), None),
            P(("rep", "wide")),
        ),
        check_vma=False,
    )
```

time: 536 us -> 196 us (0.37)
  waiting for transfers between devices: 452 us -> 78.5 us
  Pallas kernels: 0 us -> 53.7 us
  starting transfers between devices: 5.79 us -> 58.4 us
  other arithmetic: 34.9 us -> 2.33 us
  matrix products: 16.6 us -> 0 us
  between operations: 14.1 us -> 1.07 us
  local copies, waits for them, and re-layouts: 12.3 us -> 1.51 us
    all_to_all x1 -> x0, waiting for transfers between devices: 363 us -> none  [shards(): lax.all_to_all(outgoing, 'wide', split_axis=0, concat_axis=2, tiled=True)]
    reduce_scatter x1 -> x0, waiting for transfers between devices: 88.6 us -> none  [shards(): lax.psum_scatter(grad_parts[0].astype(jnp.bfloat16), 'rep', scatter_dimen...]
    ppermute x0 -> x31, waiting for transfers between devices: none -> 78.5 us  [the longest x14 44.8 us: turn_by(): return lax.ppermute(value, 'wide', pairs)]
    ppermute x0 -> x31, starting transfers between devices: none -> 58.4 us  [the longest x14 42.5 us: turn_by(): return lax.ppermute(value, 'wide', pairs)]
    pallas_call x0 -> x24, Pallas kernels: none -> 53.7 us  [the longest x4 23.2 us: update_chunk(): pl.pallas_call(functools.partial(update_kernel, start, first_chunk, last_...]
    convert_element_type x2 -> x1, other arithmetic: 18.1 us -> 0.11 us  [line_shards(): pick_both = matched.reshape(2 * capacity, rows).astype(jnp.bfloat16)]
    dot_general x1 -> x0, matrix products: 16.6 us -> none  [shards(): jnp.dot(routing.astype(jnp.float32), new_param, preferred_element_type=jn...]
    unnamed x7 -> x10, local copies, waits for them, and re-layouts: 12.3 us -> 0.69 us
  transfers between devices with their start and end apart: 2 -> 31, of which waited for: 2 -> 13; matrix products, arithmetic and copies ran while one was open for 0% -> 1% of each run, Pallas kernels for 0% -> 22%
where the time goes in v1:
time: 196 us
  waiting for transfers between devices  78.5 us (40%)
  starting transfers between devices  58.4 us (30%)
  Pallas kernels  53.7 us (27%)
  other arithmetic  2.33 us (1%)
    ppermute x14, waiting for transfers between devices, turn_by(): return lax.ppermute(value, 'wide', pairs)  44.8 us
    ppermute x14, starting transfers between devices, turn_by(): return lax.ppermute(value, 'wide', pairs)  42.5 us
    ppermute x12, waiting for transfers between devices, swap(): return lax.ppermute(value, 'rep', [(i, i ^ mask) for i in range(n_rep)])  32.3 us
    pallas_call x4, Pallas kernels, update_chunk(): pl.pallas_call(functools.partial(update_kernel, start, first_chunk, last_...  23.2 us
    ppermute x12, starting transfers between devices, swap(): return lax.ppermute(value, 'rep', [(i, i ^ mask) for i in range(n_rep)])  15 us
    pallas_call x4, Pallas kernels, cast_shares(): pl.pallas_call(functools.partial(cast_kernel, start), in_specs=[SMEM, ANY...  10.2 us
    pallas_call x4, Pallas kernels, store_rows(): pl.pallas_call(functools.partial(store_kernel, start, width), in_specs=[S...  10.1 us
    pallas_call x4, Pallas kernels, pick_rows(): pl.pallas_call(functools.partial(pick_kernel, n_sources), in_specs=[VMEM]...  9.28 us
  transfers between devices with their start and end apart: 31, of which 13 were waited for; matrix products, arithmetic and copies ran while one was open for 1% of the time, Pallas kernels for 22%

profile of v1, /device:TPU:0, one launch (start us, length us, event | category | flops | bytes accessed | tf_op | source)
XLA Modules:
  0.0 195.6 jit_solution(4851997707561958506)
XLA Ops:
  0.6 0.7 broadcast_xor_fusion.groups_ref
  1.3 2.5 %cast_shares.4 = (bf16[512,512]{1,0:T(8,128)(2,1)S(1)}, bf16[512,512]{1,0:T(8,128)(2,1)S(1)}, bf16[512,512]{1,0:T(8,128)(2,1)S(1)}) custom-call(s32[3]{0:T(128)S(1)} %broadcast_xor_fusion.groups_ref, f32[2048,2048]{1,0:T(8,128)} %bitcast.17), custom_call_target="tpu_custom_call" | custom-call | bytes 1024 | tf_op jit(solution)/shard_map/cast_shares/pallas_call | solution.py:80
  3.9 3.0 %collective-permute-start.1 = (bf16[512,512]{1,0:T(8,128)(2,1)S(1)}, bf16[512,512]{1,0:T(8,128)(2,1)S(1)}, u32[]{:S(2)}, u32[]{:S(2)}) collective-permute-start(bf16[512,512]{1,0:T(8,128)(2,1)S(1)} %get-tuple-element.71), channel_id=1, source_target_pairs={{0,16},{8,24},{16,0},{24,8},{1,17},{9,25},{17,1},{25,9},{2,18},{10... | collective-permute-start | bytes 1572872 | tf_op jit(solution)/shard_map/ppermute | solution.py:379
  6.9 1.4 collective-permute-start.2
  9.1 0.7 compare_select_fusion
  11.0 2.5 %cast_shares.5 = (bf16[512,512]{1,0:T(8,128)(2,1)S(1)}, bf16[512,512]{1,0:T(8,128)(2,1)S(1)}, bf16[512,512]{1,0:T(8,128)(2,1)S(1)}) custom-call(s32[3]{0:T(128)S(1)} %broadcast_xor_fusion.groups_ref, f32[2048,2048]{1,0:T(8,128)} %bitcast.18, bf16[512,512]{1,0:T(8,128)(2,1)S(1)} %get-tuple-element.66.refs_0_, bf16[512,512]{1,0:T(8,128)(2,1)S(1)} %bitcast.10, ...), custom_call_target="tpu_custom_call" | custom-call | bytes 1024 | tf_op jit(solution)/shard_map/cast_shares/pallas_call | solution.py:80
  13.5 16.5 %collective-permute-done.1.refs_1_ = bf16[512,512]{1,0:T(8,128)(2,1)S(1)} collective-permute-done((bf16[512,512]{1,0:T(8,128)(2,1)S(1)}, bf16[512,512]{1,0:T(8,128)(2,1)S(1)}, u32[]{:S(2)}, u32[]{:S(2)}) %collective-permute-start.1) | collective-permute-done | bytes 524320 | tf_op jit(solution)/shard_map/ppermute | solution.py:379
  30.1 1.3 collective-permute-done.refs_0_
  31.4 5.6 %update_chunk.4 = (f32[512,2048]{1,0:T(8,128)}, f32[512,2048]{1,0:T(8,128)}, f32[512,2048]{1,0:T(8,128)}, f32[512,128]{1,0:T(8,128)S(1)}, bf16[512,512]{1,0:T(8,128)(2,1)S(1)}) custom-call(s32[1]{0:T(128)} %bitcast.group_ref, f32[2048,2048]{1,0:T(8,128)} %bitcast.19, bf16[512,512]{1,0:T(8,128)(2,1)S(1)} %collective-permute-done.refs_0_, ...), custom_call_target="tpu_custom_call" | custom-call | bytes 1024 | tf_op jit(solution)/shard_map/update_chunk/pallas_call | solution.py:169
  37.0 1.8 collective-permute-start.6
  38.7 1.5 collective-permute-start.4
  40.2 1.4 collective-permute-start.5
  42.2 1.2 collective-permute-start.7
  43.4 8.8 %collective-permute-done.6.refs_11_.refs_1_ = bf16[512,512]{1,0:T(8,128)(2,1)S(1)} collective-permute-done((bf16[512,512]{1,0:T(8,128)(2,1)S(1)}, bf16[512,512]{1,0:T(8,128)(2,1)S(1)}, u32[]{:S(2)}, u32[]{:S(2)}) %collective-permute-start.6) | collective-permute-done | bytes 524320 | tf_op jit(solution)/shard_map/ppermute | solution.py:388
  52.2 10.7 %collective-permute-start.8 = (bf16[512,512]{1,0:T(8,128)(2,1)S(1)}, bf16[512,512]{1,0:T(8,128)(2,1)S(1)}, u32[]{:S(2)}, u32[]{:S(2)}) collective-permute-start(bf16[512,512]{1,0:T(8,128)(2,1)S(1)} %collective-permute-done.6.refs_11_.refs_1_), channel_id=1, source_target_pairs={{0,2},{1,3},{2,6},{3,7},{6,4},{7,5},{4,0},{5,1},{8,10},{9,11},{10,... | collective-permute-start | bytes 1572872 | tf_op jit(solution)/shard_map/ppermute | solution.py:388
  62.9 2.5 %cast_shares.6 = (bf16[512,512]{1,0:T(8,128)(2,1)S(1)}, bf16[512,512]{1,0:T(8,128)(2,1)S(1)}, bf16[512,512]{1,0:T(8,128)(2,1)S(1)}) custom-call(s32[3]{0:T(128)S(1)} %broadcast_xor_fusion.groups_ref, f32[2048,2048]{1,0:T(8,128)} %bitcast.20, bf16[512,512]{1,0:T(8,128)(2,1)S(1)} %get-tuple-element.74.refs_0_), custom_call_target="tpu_custom_call" | custom-call | bytes 1024 | tf_op jit(solution)/shard_map/cast_shares/pallas_call | solution.py:80
  65.5 5.9 %update_chunk.5 = (f32[512,2048]{1,0:T(8,128)}, f32[512,2048]{1,0:T(8,128)}, f32[512,2048]{1,0:T(8,128)}, f32[512,128]{1,0:T(8,128)S(1)}, bf16[512,512]{1,0:T(8,128)(2,1)S(1)}) custom-call(s32[1]{0:T(128)} %bitcast.group_ref, f32[2048,2048]{1,0:T(8,128)} %bitcast.21, ...), custom_call_target="tpu_custom_call", output_to_operand_aliasing={{0}: (9, {}), {1}: (10, {}), {2}: (11, {})} | custom-call | bytes 1024 | tf_op jit(solution)/shard_map/update_chunk/pallas_call | solution.py:169
  71.5 3.9 %collective-permute-start.12 = (bf16[512,512]{1,0:T(8,128)(2,1)S(1)}, bf16[512,512]{1,0:T(8,128)(2,1)S(1)}, u32[]{:S(2)}, u32[]{:S(2)}) collective-permute-start(bf16[512,512]{1,0:T(8,128)(2,1)S(1)} %get-tuple-element.84.refs_3_.refs_0_), channel_id=1, source_target_pairs={{0,2},{1,3},{2,6},{3,7},{6,4},{7,5},{4,0},{5,1},{8,10},{9,11},{10,... | collective-permute-start | bytes 1572872 | tf_op jit(solution)/shard_map/ppermute | solution.py:388
  75.4 1.5 collective-permute-start.10
  76.9 1.4 collective-permute-start.11
  78.9 16.4 %collective-permute-done.12.refs_11_.refs_1_ = bf16[512,512]{1,0:T(8,128)(2,1)S(1)} collective-permute-done((bf16[512,512]{1,0:T(8,128)(2,1)S(1)}, bf16[512,512]{1,0:T(8,128)(2,1)S(1)}, u32[]{:S(2)}, u32[]{:S(2)}) %collective-permute-start.12) | collective-permute-done | bytes 524320 | tf_op jit(solution)/shard_map/ppermute | solution.py:388
  95.3 2.5 %cast_shares.7 = (bf16[512,512]{1,0:T(8,128)(2,1)S(1)}, bf16[512,512]{1,0:T(8,128)(2,1)S(1)}, bf16[512,512]{1,0:T(8,128)(2,1)S(1)}) custom-call(s32[3]{0:T(128)S(1)} %broadcast_xor_fusion.groups_ref, f32[2048,2048]{1,0:T(8,128)} %bitcast.22, bf16[512,512]{1,0:T(8,128)(2,1)S(1)} %get-tuple-element.85.refs_0_), custom_call_target="tpu_custom_call" | custom-call | bytes 1024 | tf_op jit(solution)/shard_map/cast_shares/pallas_call | solution.py:80
  97.8 1.2 collective-permute-done.13.refs_12_.refs_2_
  99.6 5.9 %update_chunk.6 = (f32[512,2048]{1,0:T(8,128)}, f32[512,2048]{1,0:T(8,128)}, f32[512,2048]{1,0:T(8,128)}, f32[512,128]{1,0:T(8,128)S(1)}, bf16[512,512]{1,0:T(8,128)(2,1)S(1)}) custom-call(s32[1]{0:T(128)} %bitcast.group_ref, f32[2048,2048]{1,0:T(8,128)} %bitcast.23, ...), custom_call_target="tpu_custom_call", output_to_operand_aliasing={{0}: (9, {}), {1}: (10, {}), {2}: (11, {})} | custom-call | bytes 1024 | tf_op jit(solution)/shard_map/update_chunk/pallas_call | solution.py:169
  105.6 2.7 %collective-permute-done.14.refs_4_.refs_3_ = bf16[512,512]{1,0:T(8,128)(2,1)S(1)} collective-permute-done((bf16[512,512]{1,0:T(8,128)(2,1)S(1)}, bf16[512,512]{1,0:T(8,128)(2,1)S(1)}, u32[]{:S(2)}, u32[]{:S(2)}) %collective-permute-start.14) | collective-permute-done | bytes 524320 | tf_op jit(solution)/shard_map/ppermute | solution.py:388
  108.2 1.7 collective-permute-start.16
  109.9 1.4 collective-permute-start.17
  111.7 2.9 %collective-permute-start.19 = (bf16[512,512]{1,0:T(8,128)(2,1)S(1)}, bf16[512,512]{1,0:T(8,128)(2,1)S(1)}, u32[]{:S(2)}, u32[]{:S(2)}) collective-permute-start(bf16[512,512]{1,0:T(8,128)(2,1)S(1)} %get-tuple-element.95.refs_3_.refs_0_), channel_id=1, source_target_pairs={{0,4},{1,5},{2,0},{3,1},{6,2},{7,3},{4,6},{5,7},{8,12},{9,13},{10,... | collective-permute-start | bytes 1572872 | tf_op jit(solution)/shard_map/ppermute | solution.py:388
  114.6 2.2 %pick_rows.4 = (bf16[4,256,512]{2,1,0:T(8,128)(2,1)S(1)}, bf16[4,256,512]{2,1,0:T(8,128)(2,1)S(1)}) custom-call(bf16[512,512]{1,0:T(8,128)(2,1)S(1)} %bitcast.11, bf16[512,512]{1,0:T(8,128)(2,1)S(1)} %get-tuple-element.73.refs_3_.refs_0_, bf16[512,512]{1,0:T(8,128)(2,1)S(1)} %collective-permute-done.6.refs_11_.refs_1_, ...), custom_call_target="tpu_custom_call" | custom-call | bytes 1024 | tf_op jit(solution)/shard_map/pick_rows/pallas_call | solution.py:263
  116.8 13.8 %collective-permute-done.16.refs_1_ = bf16[512,512]{1,0:T(8,128)(2,1)S(1)} collective-permute-done((bf16[512,512]{1,0:T(8,128)(2,1)S(1)}, bf16[512,512]{1,0:T(8,128)(2,1)S(1)}, u32[]{:S(2)}, u32[]{:S(2)}) %collective-permute-start.16) | collective-permute-done | bytes 524320 | tf_op jit(solution)/shard_map/ppermute | solution.py:379
  130.6 2.8 %pick_rows.5 = (bf16[4,256,512]{2,1,0:T(8,128)(2,1)S(1)}, bf16[4,256,512]{2,1,0:T(8,128)(2,1)}) custom-call(bf16[512,512]{1,0:T(8,128)(2,1)S(1)} %bitcast.12, bf16[512,512]{1,0:T(8,128)(2,1)S(1)} %get-tuple-element.84.refs_3_.refs_0_, bf16[512,512]{1,0:T(8,128)(2,1)S(1)} %collective-permute-done.12.refs_11_.refs_1_, ...), custom_call_target="tpu_custom_call" | custom-call | bytes 1024 | tf_op jit(solution)/shard_map/pick_rows/pallas_call | solution.py:263
  134.0 5.8 %update_chunk.7 = (f32[512,2048]{1,0:T(8,128)}, f32[512,2048]{1,0:T(8,128)}, f32[512,2048]{1,0:T(8,128)}, f32[512,128]{1,0:T(8,128)}, bf16[528,512]{1,0:T(8,128)(2,1)S(1)}, /*index=5*/f32[8,512]{1,0:T(8,128)S(1)}) custom-call(s32[1]{0:T(128)} %bitcast.group_ref, f32[2048,2048]{1,0:T(8,128)} %bitcast.24, ...), custom_call_target="tpu_custom_call", output_to_operand_aliasing={{0}: (9, {}), {1}: (10, {}), {2}: (11, {})} | custom-call | bytes 1024 | tf_op jit(solution)/shard_map/update_chunk/pallas_call | solution.py:169
  139.8 3.0 %collective-permute-start.23 = (bf16[528,512]{1,0:T(8,128)(2,1)S(1)}, bf16[528,512]{1,0:T(8,128)(2,1)S(1)}, u32[]{:S(2)}, u32[]{:S(2)}) collective-permute-start(bf16[528,512]{1,0:T(8,128)(2,1)S(1)} %get-tuple-element.108.refs_1_.refs_0_), channel_id=1, source_target_pairs={{0,4},{1,5},{2,0},{3,1},{6,2},{7,3},{4,6},{5,7},{8,12},{9,13},{10,... | collective-permute-start | bytes 1622024 | tf_op jit(solution)/shard_map/ppermute | solution.py:388
  142.8 1.3 collective-permute-start.22
  144.1 6.1 %collective-permute-done.20.refs_2_.refs_3_ = bf16[512,512]{1,0:T(8,128)(2,1)S(1)} collective-permute-done((bf16[512,512]{1,0:T(8,128)(2,1)S(1)}, bf16[512,512]{1,0:T(8,128)(2,1)S(1)}, u32[]{:S(2)}, u32[]{:S(2)}) %collective-permute-start.20) | collective-permute-done | bytes 524320 | tf_op jit(solution)/shard_map/ppermute | solution.py:388
  150.1 14.7 %collective-permute-start.21 = (f32[8,512]{1,0:T(8,128)S(1)}, f32[8,512]{1,0:T(8,128)S(1)}, u32[]{:S(2)}, u32[]{:S(2)}) collective-permute-start(f32[8,512]{1,0:T(8,128)S(1)} %get-tuple-element.109.high_ref), channel_id=1, source_target_pairs={{0,6},{1,7},{2,4},{3,5},{6,0},{7,1},{4,2},{5,3},{8,14},{9,15},{10,... | collective-permute-start | bytes 49160 | tf_op jit(solution)/shard_map/ppermute | solution.py:388
  164.9 2.2 %pick_rows.6 = (bf16[4,256,512]{2,1,0:T(8,128)(2,1)S(1)}, bf16[4,256,512]{2,1,0:T(8,128)(2,1)S(1)}) custom-call(bf16[512,512]{1,0:T(8,128)(2,1)S(1)} %bitcast.13, bf16[512,512]{1,0:T(8,128)(2,1)S(1)} %get-tuple-element.95.refs_3_.refs_0_, bf16[512,512]{1,0:T(8,128)(2,1)S(1)} %pass_after.8.refs_10_.refs_11_.refs_1_, ...), custom_call_target="tpu_custom_call" | custom-call | bytes 16777216 | tf_op jit(solution)/shard_map/pick_rows/pallas_call | solution.py:263
  167.1 6.3 %collective-permute-done.21.across_ref = f32[8,512]{1,0:T(8,128)S(1)} collective-permute-done((f32[8,512]{1,0:T(8,128)S(1)}, f32[8,512]{1,0:T(8,128)S(1)}, u32[]{:S(2)}, u32[]{:S(2)}) %collective-permute-start.21) | collective-permute-done | bytes 16416 | tf_op jit(solution)/shard_map/ppermute | solution.py:388
  173.7 2.8 %collective-permute-start.26 = (bf16[512,256]{1,0:T(8,128)(2,1)S(1)}, bf16[512,256]{1,0:T(8,128)(2,1)S(1)}, u32[]{:S(2)}, u32[]{:S(2)}) collective-permute-start(bf16[512,256]{1,0:T(8,128)(2,1)S(1)} %get-tuple-element.112.refs_3_), channel_id=1, source_target_pairs={{0,4},{1,5},{2,0},{3,1},{6,2},{7,3},{4,6},{5,7},{8,12},{9,13},{10,... | collective-permute-start | bytes 786440 | tf_op jit(solution)/shard_map/ppermute | solution.py:388
  176.5 1.2 collective-permute-done.24.refs_1_
  177.8 0.7 slot_scales.1
  178.6 0.7 copy-done
  179.2 2.4 %store_rows.4 = (bf16[256,16384]{1,0:T(8,128)(2,1)}, f32[8,128]{1,0:T(8,128)S(1)}) custom-call(s32[8]{0:T(128)S(1)} %pass_after.9.refs_4_.place_ref, f32[256,1]{1,0:T(8,128)S(1)} %get-tuple-element.113.inverse_ref, bf16[4,256,512]{2,1,0:T(8,128)(2,1)S(1)} %get-tuple-element.103.refs_4_.mine_ref, bf16[4,256,512]{2,1,0:T(8,128)(2,1)S(1)} %collective-permute-done.28.other_ref, ...), custom_call_target="tpu_custom_call" | custom-call | bytes 1024 | tf_op jit(solution)/shard_map/store_rows/pallas_call | solution.py:297
  181.6 2.4 %store_rows.5 = (bf16[256,16384]{1,0:T(8,128)(2,1)}, f32[8,128]{1,0:T(8,128)S(1)}) custom-call(s32[8]{0:T(128)S(1)} %pass_after.9.refs_4_.place_ref, f32[256,1]{1,0:T(8,128)S(1)} %get-tuple-element.113.inverse_ref, bf16[4,256,512]{2,1,0:T(8,128)(2,1)S(1)} %get-tuple-element.104.refs_1_.mine_ref, ...), custom_call_target="tpu_custom_call", output_to_operand_aliasing={{0}: (4, {})} | custom-call | bytes 1024 | tf_op jit(solution)/shard_map/store_rows/pallas_call | solution.py:297
  184.0 3.5 %collective-permute-done.26.refs_4_ = bf16[512,256]{1,0:T(8,128)(2,1)S(1)} collective-permute-done((bf16[512,256]{1,0:T(8,128)(2,1)S(1)}, bf16[512,256]{1,0:T(8,128)(2,1)S(1)}, u32[]{:S(2)}, u32[]{:S(2)}) %collective-permute-start.26) | collective-permute-done | bytes 262176 | tf_op jit(solution)/shard_map/ppermute | solution.py:388
  187.5 2.2 %pick_rows.7 = (bf16[4,256,512]{2,1,0:T(8,128)(2,1)S(1)}, bf16[4,256,512]{2,1,0:T(8,128)(2,1)S(1)}) custom-call(bf16[512,512]{1,0:T(8,128)(2,1)S(1)} %bitcast.15, bf16[528,512]{1,0:T(8,128)(2,1)S(1)} %get-tuple-element.108.refs_1_.refs_0_, bf16[528,512]{1,0:T(8,128)(2,1)S(1)} %collective-permute-done.22.ahead_ref.refs_1_, ...), custom_call_target="tpu_custom_call" | custom-call | bytes 1024 | tf_op jit(solution)/shard_map/pick_rows/pallas_call | solution.py:263
  189.8 2.4 %store_rows.6 = (bf16[256,16384]{1,0:T(8,128)(2,1)}, f32[8,128]{1,0:T(8,128)S(1)}) custom-call(s32[8]{0:T(128)S(1)} %pass_after.9.refs_4_.place_ref, f32[256,1]{1,0:T(8,128)S(1)} %get-tuple-element.113.inverse_ref, bf16[4,256,512]{2,1,0:T(8,128)(2,1)S(1)} %get-tuple-element.110.refs_0_.mine_ref, ...), custom_call_target="tpu_custom_call", output_to_operand_aliasing={{0}: (4, {})} | custom-call | bytes 1024 | tf_op jit(solution)/shard_map/store_rows/pallas_call | solution.py:297
  192.4 3.0 %store_rows.7 = (bf16[256,16384]{1,0:T(8,128)(2,1)}, f32[8,128]{1,0:T(8,128)}) custom-call(s32[8]{0:T(128)S(1)} %pass_after.9.refs_4_.place_ref, f32[256,1]{1,0:T(8,128)S(1)} %get-tuple-element.113.inverse_ref, bf16[4,256,512]{2,1,0:T(8,128)(2,1)S(1)} %get-tuple-element.120.refs_1_.mine_ref, ...), custom_call_target="tpu_custom_call", output_to_operand_aliasing={{0}: (4, {})} | custom-call | bytes 1024 | tf_op jit(solution)/shard_map/store_rows/pallas_call | solution.py:297
  (61 shorter events, 5.5 us)
Async XLA Ops:
  1.3 7.1 %copy-start.1 = (s32[4]{0:T(128)S(1)}, s32[4]{0:T(128)}, u32[]{:S(2)}) copy-start(s32[4]{0:T(128)} %constant.64.clone) | copy-start | bytes 52
  1.3 7.8 %copy-start.4 = (s32[4]{0:T(128)S(1)}, s32[4]{0:T(128)}, u32[]{:S(2)}) copy-start(s32[4]{0:T(128)} %constant.65.clone) | copy-start | bytes 52
  1.3 9.2 %copy-start.3 = (s32[512]{0:T(512)S(1)}, s32[512]{0:T(512)}, u32[]{:S(2)}) copy-start(s32[512]{0:T(512)} %param.17) | copy-start | bytes 6148
  1.3 9.5 %copy-start.2 = (s32[512]{0:T(512)S(1)}, s32[512]{0:T(512)}, u32[]{:S(2)}) copy-start(s32[512]{0:T(512)} %param.18) | copy-start | bytes 6148
  3.9 26.2 %collective-permute-start.1 = (bf16[512,512]{1,0:T(8,128)(2,1)S(1)}, bf16[512,512]{1,0:T(8,128)(2,1)S(1)}, u32[]{:S(2)}, u32[]{:S(2)}) collective-permute-start(bf16[512,512]{1,0:T(8,128)(2,1)S(1)} %get-tuple-element.71), channel_id=1, source_target_pairs={{0,16},{8,24},{16,0},{24,8},{1,17},{9,25},{17,1},{25,9},{2,18},{10... | collective-permute-start | bytes 1572872 | tf_op jit(solution)/shard_map/ppermute | solution.py:379
  6.9 23.2 %collective-permute-start.2 = (bf16[512,512]{1,0:T(8,128)(2,1)S(1)}, bf16[512,512]{1,0:T(8,128)(2,1)S(1)}, u32[]{:S(2)}, u32[]{:S(2)}) collective-permute-start(bf16[512,512]{1,0:T(8,128)(2,1)S(1)} %get-tuple-element.72), channel_id=1, source_target_pairs={{0,24},{8,16},{16,8},{24,0},{1,25},{9,17},{17,9},{25,1},{2,26},{10... | collective-permute-start | bytes 1572872 | tf_op jit(solution)/shard_map/ppermute | solution.py:379
  8.3 23.0 %collective-permute-start = (bf16[512,512]{1,0:T(8,128)(2,1)S(1)}, bf16[512,512]{1,0:T(8,128)(2,1)S(1)}, u32[]{:S(2)}, u32[]{:S(2)}) collective-permute-start(bf16[512,512]{1,0:T(8,128)(2,1)S(1)} %get-tuple-element.66.refs_0_), channel_id=1, source_target_pairs={{0,8},{8,0},{16,24},{24,16},{1,9},{9,1},{17,25},{25,17},{2,10},{10... | collective-permute-start | bytes 1572872 | tf_op jit(solution)/shard_map/ppermute | solution.py:379
  37.0 15.3 %collective-permute-start.6 = (bf16[512,512]{1,0:T(8,128)(2,1)S(1)}, bf16[512,512]{1,0:T(8,128)(2,1)S(1)}, u32[]{:S(2)}, u32[]{:S(2)}) collective-permute-start(bf16[512,512]{1,0:T(8,128)(2,1)S(1)} %get-tuple-element.73.refs_3_.refs_0_), channel_id=1, source_target_pairs={{0,2},{1,3},{2,6},{3,7},{6,4},{7,5},{4,0},{5,1},{8,10},{9,11},{10,... | collective-permute-start | bytes 1572872 | tf_op jit(solution)/shard_map/ppermute | solution.py:388
  38.7 26.8 %collective-permute-start.4 = (bf16[512,512]{1,0:T(8,128)(2,1)S(1)}, bf16[512,512]{1,0:T(8,128)(2,1)S(1)}, u32[]{:S(2)}, u32[]{:S(2)}) collective-permute-start(bf16[512,512]{1,0:T(8,128)(2,1)S(1)} %get-tuple-element.78), channel_id=1, source_target_pairs={{0,16},{8,24},{16,0},{24,8},{1,17},{9,25},{17,1},{25,9},{2,18},{10... | collective-permute-start | bytes 1572872 | tf_op jit(solution)/shard_map/ppermute | solution.py:379
  40.2 25.2 %collective-permute-start.5 = (bf16[512,512]{1,0:T(8,128)(2,1)S(1)}, bf16[512,512]{1,0:T(8,128)(2,1)S(1)}, u32[]{:S(2)}, u32[]{:S(2)}) collective-permute-start(bf16[512,512]{1,0:T(8,128)(2,1)S(1)} %get-tuple-element.79), channel_id=1, source_target_pairs={{0,24},{8,16},{16,8},{24,0},{1,25},{9,17},{17,9},{25,1},{2,26},{10... | collective-permute-start | bytes 1572872 | tf_op jit(solution)/shard_map/ppermute | solution.py:379
  41.7 23.8 %collective-permute-start.3 = (bf16[512,512]{1,0:T(8,128)(2,1)S(1)}, bf16[512,512]{1,0:T(8,128)(2,1)S(1)}, u32[]{:S(2)}, u32[]{:S(2)}) collective-permute-start(bf16[512,512]{1,0:T(8,128)(2,1)S(1)} %get-tuple-element.74.refs_0_), channel_id=1, source_target_pairs={{0,8},{8,0},{16,24},{24,16},{1,9},{9,1},{17,25},{25,17},{2,10},{10... | collective-permute-start | bytes 1572872 | tf_op jit(solution)/shard_map/ppermute | solution.py:379
  42.2 23.3 %collective-permute-start.7 = (bf16[512,512]{1,0:T(8,128)(2,1)S(1)}, bf16[512,512]{1,0:T(8,128)(2,1)S(1)}, u32[]{:S(2)}, u32[]{:S(2)}) collective-permute-start(bf16[512,512]{1,0:T(8,128)(2,1)S(1)} %get-tuple-element.73.refs_3_.refs_0_), channel_id=1, source_target_pairs={{0,4},{1,5},{2,0},{3,1},{6,2},{7,3},{4,6},{5,7},{8,12},{9,13},{10,... | collective-permute-start | bytes 1572872 | tf_op jit(solution)/shard_map/ppermute | solution.py:388
  52.2 23.2 %collective-permute-start.8 = (bf16[512,512]{1,0:T(8,128)(2,1)S(1)}, bf16[512,512]{1,0:T(8,128)(2,1)S(1)}, u32[]{:S(2)}, u32[]{:S(2)}) collective-permute-start(bf16[512,512]{1,0:T(8,128)(2,1)S(1)} %collective-permute-done.6.refs_11_.refs_1_), channel_id=1, source_target_pairs={{0,2},{1,3},{2,6},{3,7},{6,4},{7,5},{4,0},{5,1},{8,10},{9,11},{10,... | collective-permute-start | bytes 1572872 | tf_op jit(solution)/shard_map/ppermute | solution.py:388
  71.5 23.8 %collective-permute-start.12 = (bf16[512,512]{1,0:T(8,128)(2,1)S(1)}, bf16[512,512]{1,0:T(8,128)(2,1)S(1)}, u32[]{:S(2)}, u32[]{:S(2)}) collective-permute-start(bf16[512,512]{1,0:T(8,128)(2,1)S(1)} %get-tuple-element.84.refs_3_.refs_0_), channel_id=1, source_target_pairs={{0,2},{1,3},{2,6},{3,7},{6,4},{7,5},{4,0},{5,1},{8,10},{9,11},{10,... | collective-permute-start | bytes 1572872 | tf_op jit(solution)/shard_map/ppermute | solution.py:388
  75.4 23.6 %collective-permute-start.13 = (bf16[512,512]{1,0:T(8,128)(2,1)S(1)}, bf16[512,512]{1,0:T(8,128)(2,1)S(1)}, u32[]{:S(2)}, u32[]{:S(2)}) collective-permute-start(bf16[512,512]{1,0:T(8,128)(2,1)S(1)} %get-tuple-element.84.refs_3_.refs_0_), channel_id=1, source_target_pairs={{0,4},{1,5},{2,0},{3,1},{6,2},{7,3},{4,6},{5,7},{8,12},{9,13},{10,... | collective-permute-start | bytes 1572872 | tf_op jit(solution)/shard_map/ppermute | solution.py:388
  75.4 23.6 %collective-permute-start.10 = (bf16[512,512]{1,0:T(8,128)(2,1)S(1)}, bf16[512,512]{1,0:T(8,128)(2,1)S(1)}, u32[]{:S(2)}, u32[]{:S(2)}) collective-permute-start(bf16[512,512]{1,0:T(8,128)(2,1)S(1)} %get-tuple-element.89), channel_id=1, source_target_pairs={{0,16},{8,24},{16,0},{24,8},{1,17},{9,25},{17,1},{25,9},{2,18},{10... | collective-permute-start | bytes 1572872 | tf_op jit(solution)/shard_map/ppermute | solution.py:379
  76.9 22.1 %collective-permute-start.11 = (bf16[512,512]{1,0:T(8,128)(2,1)S(1)}, bf16[512,512]{1,0:T(8,128)(2,1)S(1)}, u32[]{:S(2)}, u32[]{:S(2)}) collective-permute-start(bf16[512,512]{1,0:T(8,128)(2,1)S(1)} %get-tuple-element.90), channel_id=1, source_target_pairs={{0,24},{8,16},{16,8},{24,0},{1,25},{9,17},{17,9},{25,1},{2,26},{10... | collective-permute-start | bytes 1572872 | tf_op jit(solution)/shard_map/ppermute | solution.py:379
  78.3 21.3 %collective-permute-start.9 = (bf16[512,512]{1,0:T(8,128)(2,1)S(1)}, bf16[512,512]{1,0:T(8,128)(2,1)S(1)}, u32[]{:S(2)}, u32[]{:S(2)}) collective-permute-start(bf16[512,512]{1,0:T(8,128)(2,1)S(1)} %get-tuple-element.85.refs_0_), channel_id=1, source_target_pairs={{0,8},{8,0},{16,24},{24,16},{1,9},{9,1},{17,25},{25,17},{2,10},{10... | collective-permute-start | bytes 1572872 | tf_op jit(solution)/shard_map/ppermute | solution.py:379
  95.3 13.0 %collective-permute-start.14 = (bf16[512,512]{1,0:T(8,128)(2,1)S(1)}, bf16[512,512]{1,0:T(8,128)(2,1)S(1)}, u32[]{:S(2)}, u32[]{:S(2)}) collective-permute-start(bf16[512,512]{1,0:T(8,128)(2,1)S(1)} %collective-permute-done.12.refs_11_.refs_1_), channel_id=1, source_target_pairs={{0,2},{1,3},{2,6},{3,7},{6,4},{7,5},{4,0},{5,1},{8,10},{9,11},{10,... | collective-permute-start | bytes 1572872 | tf_op jit(solution)/shard_map/ppermute | solution.py:388
  108.2 22.4 %collective-permute-start.16 = (bf16[512,512]{1,0:T(8,128)(2,1)S(1)}, bf16[512,512]{1,0:T(8,128)(2,1)S(1)}, u32[]{:S(2)}, u32[]{:S(2)}) collective-permute-start(bf16[512,512]{1,0:T(8,128)(2,1)S(1)} %get-tuple-element.97), channel_id=1, source_target_pairs={{0,16},{8,24},{16,0},{24,8},{1,17},{9,25},{17,1},{25,9},{2,18},{10... | collective-permute-start | bytes 1572872 | tf_op jit(solution)/shard_map/ppermute | solution.py:379
  109.9 23.5 %collective-permute-start.18 = (bf16[512,512]{1,0:T(8,128)(2,1)S(1)}, bf16[512,512]{1,0:T(8,128)(2,1)S(1)}, u32[]{:S(2)}, u32[]{:S(2)}) collective-permute-start(bf16[512,512]{1,0:T(8,128)(2,1)S(1)} %get-tuple-element.95.refs_3_.refs_0_), channel_id=1, source_target_pairs={{0,2},{1,3},{2,6},{3,7},{6,4},{7,5},{4,0},{5,1},{8,10},{9,11},{10,... | collective-permute-start | bytes 1572872 | tf_op jit(solution)/shard_map/ppermute | solution.py:388
  109.9 24.1 %collective-permute-start.17 = (bf16[512,512]{1,0:T(8,128)(2,1)S(1)}, bf16[512,512]{1,0:T(8,128)(2,1)S(1)}, u32[]{:S(2)}, u32[]{:S(2)}) collective-permute-start(bf16[512,512]{1,0:T(8,128)(2,1)S(1)} %get-tuple-element.98), channel_id=1, source_target_pairs={{0,24},{8,16},{16,8},{24,0},{1,25},{9,17},{17,9},{25,1},{2,26},{10... | collective-permute-start | bytes 1572872 | tf_op jit(solution)/shard_map/ppermute | solution.py:379
  111.3 22.6 %collective-permute-start.15 = (bf16[512,512]{1,0:T(8,128)(2,1)S(1)}, bf16[512,512]{1,0:T(8,128)(2,1)S(1)}, u32[]{:S(2)}, u32[]{:S(2)}) collective-permute-start(bf16[512,512]{1,0:T(8,128)(2,1)S(1)} %get-tuple-element.96.refs_4_), channel_id=1, source_target_pairs={{0,8},{8,0},{16,24},{24,16},{1,9},{9,1},{17,25},{25,17},{2,10},{10... | collective-permute-start | bytes 1572872 | tf_op jit(solution)/shard_map/ppermute | solution.py:379
  111.7 22.3 %collective-permute-start.19 = (bf16[512,512]{1,0:T(8,128)(2,1)S(1)}, bf16[512,512]{1,0:T(8,128)(2,1)S(1)}, u32[]{:S(2)}, u32[]{:S(2)}) collective-permute-start(bf16[512,512]{1,0:T(8,128)(2,1)S(1)} %get-tuple-element.95.refs_3_.refs_0_), channel_id=1, source_target_pairs={{0,4},{1,5},{2,0},{3,1},{6,2},{7,3},{4,6},{5,7},{8,12},{9,13},{10,... | collective-permute-start | bytes 1572872 | tf_op jit(solution)/shard_map/ppermute | solution.py:388
  130.6 48.0 %collective-permute-start.28 = (bf16[4,256,512]{2,1,0:T(8,128)(2,1)S(1)}, bf16[4,256,512]{2,1,0:T(8,128)(2,1)S(1)}, u32[]{:S(2)}, u32[]{:S(2)}) collective-permute-start(bf16[4,256,512]{2,1,0:T(8,128)(2,1)S(1)} %get-tuple-element.115), channel_id=1, source_target_pairs={{0,1},{1,0},{2,3},{3,2},{4,5},{5,4},{6,7},{7,6},{8,9},{9,8},{10,11... | collective-permute-start | bytes 3145736 | tf_op jit(solution)/shard_map/ppermute | solution.py:391
  133.4 48.2 %collective-permute-start.27 = (bf16[4,256,512]{2,1,0:T(8,128)(2,1)}, bf16[4,256,512]{2,1,0:T(8,128)(2,1)S(1)}, u32[]{:S(2)}, u32[]{:S(2)}) collective-permute-start(bf16[4,256,512]{2,1,0:T(8,128)(2,1)} %get-tuple-element.114), channel_id=1, source_target_pairs={{0,1},{1,0},{2,3},{3,2},{4,5},{5,4},{6,7},{7,6},{8,9},{9,8},{10,11... | collective-permute-start | bytes 3145736 | tf_op jit(solution)/shard_map/ppermute | solution.py:391
  133.9 16.2 %collective-permute-start.20 = (bf16[512,512]{1,0:T(8,128)(2,1)S(1)}, bf16[512,512]{1,0:T(8,128)(2,1)S(1)}, u32[]{:S(2)}, u32[]{:S(2)}) collective-permute-start(bf16[512,512]{1,0:T(8,128)(2,1)S(1)} %pass_after.8.refs_10_.refs_11_.refs_1_), channel_id=1, source_target_pairs={{0,2},{1,3},{2,6},{3,7},{6,4},{7,5},{4,0},{5,1},{8,10},{9,11},{10,... | collective-permute-start | bytes 1572872 | tf_op jit(solution)/shard_map/ppermute | solution.py:388
  139.8 33.5 %collective-permute-start.23 = (bf16[528,512]{1,0:T(8,128)(2,1)S(1)}, bf16[528,512]{1,0:T(8,128)(2,1)S(1)}, u32[]{:S(2)}, u32[]{:S(2)}) collective-permute-start(bf16[528,512]{1,0:T(8,128)(2,1)S(1)} %get-tuple-element.108.refs_1_.refs_0_), channel_id=1, source_target_pairs={{0,4},{1,5},{2,0},{3,1},{6,2},{7,3},{4,6},{5,7},{8,12},{9,13},{10,... | collective-permute-start | bytes 1622024 | tf_op jit(solution)/shard_map/ppermute | solution.py:388
  142.8 30.6 %collective-permute-start.22 = (bf16[528,512]{1,0:T(8,128)(2,1)S(1)}, bf16[528,512]{1,0:T(8,128)(2,1)S(1)}, u32[]{:S(2)}, u32[]{:S(2)}) collective-permute-start(bf16[528,512]{1,0:T(8,128)(2,1)S(1)} %get-tuple-element.108.refs_1_.refs_0_), channel_id=1, source_target_pairs={{0,2},{1,3},{2,6},{3,7},{6,4},{7,5},{4,0},{5,1},{8,10},{9,11},{10,... | collective-permute-start | bytes 1622024 | tf_op jit(solution)/shard_map/ppermute | solution.py:388
  150.1 23.2 %collective-permute-start.21 = (f32[8,512]{1,0:T(8,128)S(1)}, f32[8,512]{1,0:T(8,128)S(1)}, u32[]{:S(2)}, u32[]{:S(2)}) collective-permute-start(f32[8,512]{1,0:T(8,128)S(1)} %get-tuple-element.109.high_ref), channel_id=1, source_target_pairs={{0,6},{1,7},{2,4},{3,5},{6,0},{7,1},{4,2},{5,3},{8,14},{9,15},{10,... | collective-permute-start | bytes 49160 | tf_op jit(solution)/shard_map/ppermute | solution.py:388
  173.5 10.5 %collective-permute-start.25 = (bf16[512,256]{1,0:T(8,128)(2,1)S(1)}, bf16[512,256]{1,0:T(8,128)(2,1)S(1)}, u32[]{:S(2)}, u32[]{:S(2)}) collective-permute-start(bf16[512,256]{1,0:T(8,128)(2,1)S(1)} %get-tuple-element.111.refs_2_), channel_id=1, source_target_pairs={{0,2},{1,3},{2,6},{3,7},{6,4},{7,5},{4,0},{5,1},{8,10},{9,11},{10,... | collective-permute-start | bytes 786440 | tf_op jit(solution)/shard_map/ppermute | solution.py:388
  173.7 13.8 %collective-permute-start.26 = (bf16[512,256]{1,0:T(8,128)(2,1)S(1)}, bf16[512,256]{1,0:T(8,128)(2,1)S(1)}, u32[]{:S(2)}, u32[]{:S(2)}) collective-permute-start(bf16[512,256]{1,0:T(8,128)(2,1)S(1)} %get-tuple-element.112.refs_3_), channel_id=1, source_target_pairs={{0,4},{1,5},{2,0},{3,1},{6,2},{7,3},{4,6},{5,7},{8,12},{9,13},{10,... | collective-permute-start | bytes 786440 | tf_op jit(solution)/shard_map/ppermute | solution.py:388
  176.5 1.2 collective-permute-start.24
  177.6 12.2 %collective-permute-start.30 = (bf16[4,256,512]{2,1,0:T(8,128)(2,1)S(1)}, bf16[4,256,512]{2,1,0:T(8,128)(2,1)S(1)}, u32[]{:S(2)}, u32[]{:S(2)}) collective-permute-start(bf16[4,256,512]{2,1,0:T(8,128)(2,1)S(1)} %get-tuple-element.122), channel_id=1, source_target_pairs={{0,1},{1,0},{2,3},{3,2},{4,5},{5,4},{6,7},{7,6},{8,9},{9,8},{10,11... | collective-permute-start | bytes 3145736 | tf_op jit(solution)/shard_map/ppermute | solution.py:391
  178.5 0.7 copy-start
  189.7 2.7 %collective-permute-start.29 = (bf16[4,256,512]{2,1,0:T(8,128)(2,1)S(1)}, bf16[4,256,512]{2,1,0:T(8,128)(2,1)S(1)}, u32[]{:S(2)}, u32[]{:S(2)}) collective-permute-start(bf16[4,256,512]{2,1,0:T(8,128)(2,1)S(1)} %get-tuple-element.121), channel_id=1, source_target_pairs={{0,1},{1,0},{2,3},{3,2},{4,5},{5,4},{6,7},{7,6},{8,9},{9,8},{10,11... | collective-permute-start | bytes 3145736 | tf_op jit(solution)/shard_map/ppermute | solution.py:391

commit v2 on v1

--- a/solution.py
+++ b/solution.py
@@ -16,8 +16,8 @@
 CHUNKS = (512, 512, 512, 512)
 ORDER = (
     ("cast", 0), ("sum", 0), ("cast", 1), ("update", 0), ("sum", 1), ("cast", 2), ("update", 1), ("sum", 2),
-    ("cast", 3), ("update", 2), ("sum", 3), ("pick", 0), ("pick", 1), ("forward", 2), ("update", 3), ("mark", 0),
-    ("pick", 2), ("peaks", 0), ("halves", 3), ("scales", 0), ("store", 0), ("store", 1), ("pick", 3), ("store", 2),
+    ("cast", 3), ("update", 2), ("sum", 3), ("pick", 0), ("pick", 1), ("update", 3), ("mark", 0), ("pick", 2),
+    ("peaks", 0), ("halves", 3), ("scales", 0), ("store", 0), ("store", 1), ("pick", 3), ("store", 2),
     ("store", 3),
 )
 
@@ -256,7 +256,7 @@
     wait_copies(leaving)
 
 
-def pick_rows(pick, sources, after, moved=1024):
+def pick_rows(pick, sources, after):
     rows, size = pick.shape[1], sources[0].shape[1]
     slots = pick.shape[0] // 2
     n_sources, n = len(sources), 4
@@ -272,7 +272,7 @@
             DMA((2 * n,)),
         ],
         compiler_params=params(),
-        cost_estimate=pl.CostEstimate(flops=0, bytes_accessed=moved, transcendentals=0),
+        cost_estimate=cost(4 * n * rows * size),
         name="pick_rows",
     )(pick, *sources, *after)
 
@@ -427,24 +427,21 @@
             after = [sent]
             ahead, back = turn_by(sent, 1), turn_by(sent, -1)
             pieces[k] = [sent, ahead, back]
-            if k < last - 1:
+            if k < last:
                 forwarded[k] = [turn_by(ahead, 1)]
-            elif k == last:
-                high, across = new[5], turn_by(new[5], 2)
-        elif kind == "forward":
-            (ahead,) = pass_after([ahead], after)
-            pieces[k] = [sent, ahead, back]
-            forwarded[k] = [turn_by(ahead, 1)]
-            after = [ahead]
+            else:
+                high = new[5]
         elif kind == "mark":
-            after = pass_after([place], after + forwarded[last - 1])
-            (place,) = after
+            (high,) = pass_after([high], after + forwarded[last - 1])
+            across = turn_by(high, 2)
+            after = [high]
         elif kind == "halves":
             after = cut_halves(ahead, back, after)
             forwarded[k] = [turn_by(half, way) for half, way in zip(after, (1, -1))]
         elif kind == "pick":
-            moved = 2**24 if k == last - 1 else 1024
-            mine, other = pick_rows(pick_both, pieces[k] + forwarded[k], after, moved)
+            if k == 0:
+                after = after + [ahead]
+            mine, other = pick_rows(pick_both, pieces[k] + forwarded[k], after)
             pieces[k] = mine, sibling(other)
             after = [mine]
         elif kind == "peaks":

time: 196 us -> 199 us (1.015)
  starting transfers between devices: 58.4 us -> 65.1 us
  waiting for transfers between devices: 78.5 us -> 75 us
    ppermute x12, waiting for transfers between devices: 32.3 us -> 24.5 us  [swap(): return lax.ppermute(value, 'rep', [(i, i ^ mask) for i in range(n_rep)])]
    ppermute x14, starting transfers between devices: 42.5 us -> 49.8 us  [turn_by(): return lax.ppermute(value, 'wide', pairs)]
    ppermute x14, waiting for transfers between devices: 44.8 us -> 49 us  [turn_by(): return lax.ppermute(value, 'wide', pairs)]
  transfers between devices with their start and end apart: 31 -> 31, of which waited for: 13 -> 14; matrix products, arithmetic and copies ran while one was open for 1% -> 1% of each run, Pallas kernels for 22% -> 21%
where the time goes in v2:
time: 199 us
  waiting for transfers between devices  75 us (38%)
  starting transfers between devices  65.1 us (33%)
  Pallas kernels  53.7 us (27%)
  other arithmetic  2.33 us (1%)
    ppermute x14, starting transfers between devices, turn_by(): return lax.ppermute(value, 'wide', pairs)  49.8 us
    ppermute x14, waiting for transfers between devices, turn_by(): return lax.ppermute(value, 'wide', pairs)  49 us
    ppermute x12, waiting for transfers between devices, swap(): return lax.ppermute(value, 'rep', [(i, i ^ mask) for i in range(n_rep)])  24.5 us
    pallas_call x4, Pallas kernels, update_chunk(): pl.pallas_call(functools.partial(update_kernel, start, first_chunk, last_...  23.2 us
    ppermute x12, starting transfers between devices, swap(): return lax.ppermute(value, 'rep', [(i, i ^ mask) for i in range(n_rep)])  15 us
    pallas_call x4, Pallas kernels, cast_shares(): pl.pallas_call(functools.partial(cast_kernel, start), in_specs=[SMEM, ANY...  10.2 us
    pallas_call x4, Pallas kernels, store_rows(): pl.pallas_call(functools.partial(store_kernel, start, width), in_specs=[S...  10.1 us
    pallas_call x4, Pallas kernels, pick_rows(): pl.pallas_call(functools.partial(pick_kernel, n_sources), in_specs=[VMEM]...  9.28 us
  transfers between devices with their start and end apart: 31, of which 14 were waited for; matrix products, arithmetic and copies ran while one was open for 1% of the time, Pallas kernels for 21%

profile of v2, /device:TPU:0, one launch (start us, length us, event | category | flops | bytes accessed | tf_op | source)
XLA Modules:
  0.0 198.7 jit_solution(8354390759092941923)
XLA Ops:
  0.6 0.7 broadcast_xor_fusion.groups_ref
  1.3 2.5 %cast_shares.4 = (bf16[512,512]{1,0:T(8,128)(2,1)S(1)}, bf16[512,512]{1,0:T(8,128)(2,1)S(1)}, bf16[512,512]{1,0:T(8,128)(2,1)S(1)}) custom-call(s32[3]{0:T(128)S(1)} %broadcast_xor_fusion.groups_ref, f32[2048,2048]{1,0:T(8,128)} %bitcast.17), custom_call_target="tpu_custom_call" | custom-call | bytes 1024 | tf_op jit(solution)/shard_map/cast_shares/pallas_call | solution.py:80
  3.9 3.0 %collective-permute-start.1 = (bf16[512,512]{1,0:T(8,128)(2,1)S(1)}, bf16[512,512]{1,0:T(8,128)(2,1)S(1)}, u32[]{:S(2)}, u32[]{:S(2)}) collective-permute-start(bf16[512,512]{1,0:T(8,128)(2,1)S(1)} %get-tuple-element.71), channel_id=1, source_target_pairs={{0,16},{8,24},{16,0},{24,8},{1,17},{9,25},{17,1},{25,9},{2,18},{10... | collective-permute-start | bytes 1572872 | tf_op jit(solution)/shard_map/ppermute | solution.py:379
  6.9 1.4 collective-permute-start.2
  9.1 0.7 compare_select_fusion
  11.0 2.5 %cast_shares.5 = (bf16[512,512]{1,0:T(8,128)(2,1)S(1)}, bf16[512,512]{1,0:T(8,128)(2,1)S(1)}, bf16[512,512]{1,0:T(8,128)(2,1)S(1)}) custom-call(s32[3]{0:T(128)S(1)} %broadcast_xor_fusion.groups_ref, f32[2048,2048]{1,0:T(8,128)} %bitcast.18, bf16[512,512]{1,0:T(8,128)(2,1)S(1)} %get-tuple-element.66.refs_0_, bf16[512,512]{1,0:T(8,128)(2,1)S(1)} %bitcast.10, ...), custom_call_target="tpu_custom_call" | custom-call | bytes 1024 | tf_op jit(solution)/shard_map/cast_shares/pallas_call | solution.py:80
  13.5 16.5 %collective-permute-done.1.refs_1_ = bf16[512,512]{1,0:T(8,128)(2,1)S(1)} collective-permute-done((bf16[512,512]{1,0:T(8,128)(2,1)S(1)}, bf16[512,512]{1,0:T(8,128)(2,1)S(1)}, u32[]{:S(2)}, u32[]{:S(2)}) %collective-permute-start.1) | collective-permute-done | bytes 524320 | tf_op jit(solution)/shard_map/ppermute | solution.py:379
  30.1 1.3 collective-permute-done.refs_0_
  31.4 5.6 %update_chunk.4 = (f32[512,2048]{1,0:T(8,128)}, f32[512,2048]{1,0:T(8,128)}, f32[512,2048]{1,0:T(8,128)}, f32[512,128]{1,0:T(8,128)S(1)}, bf16[512,512]{1,0:T(8,128)(2,1)S(1)}) custom-call(s32[1]{0:T(128)} %bitcast.group_ref, f32[2048,2048]{1,0:T(8,128)} %bitcast.19, bf16[512,512]{1,0:T(8,128)(2,1)S(1)} %collective-permute-done.refs_0_, ...), custom_call_target="tpu_custom_call" | custom-call | bytes 1024 | tf_op jit(solution)/shard_map/update_chunk/pallas_call | solution.py:169
  37.0 1.8 collective-permute-start.6
  38.7 1.5 collective-permute-start.4
  40.2 1.4 collective-permute-start.5
  42.2 1.2 collective-permute-start.7
  43.4 8.8 %collective-permute-done.6.refs_11_.refs_1_ = bf16[512,512]{1,0:T(8,128)(2,1)S(1)} collective-permute-done((bf16[512,512]{1,0:T(8,128)(2,1)S(1)}, bf16[512,512]{1,0:T(8,128)(2,1)S(1)}, u32[]{:S(2)}, u32[]{:S(2)}) %collective-permute-start.6) | collective-permute-done | bytes 524320 | tf_op jit(solution)/shard_map/ppermute | solution.py:388
  52.2 10.7 %collective-permute-start.8 = (bf16[512,512]{1,0:T(8,128)(2,1)S(1)}, bf16[512,512]{1,0:T(8,128)(2,1)S(1)}, u32[]{:S(2)}, u32[]{:S(2)}) collective-permute-start(bf16[512,512]{1,0:T(8,128)(2,1)S(1)} %collective-permute-done.6.refs_11_.refs_1_), channel_id=1, source_target_pairs={{0,2},{1,3},{2,6},{3,7},{6,4},{7,5},{4,0},{5,1},{8,10},{9,11},{10,... | collective-permute-start | bytes 1572872 | tf_op jit(solution)/shard_map/ppermute | solution.py:388
  62.9 2.5 %cast_shares.6 = (bf16[512,512]{1,0:T(8,128)(2,1)S(1)}, bf16[512,512]{1,0:T(8,128)(2,1)S(1)}, bf16[512,512]{1,0:T(8,128)(2,1)S(1)}) custom-call(s32[3]{0:T(128)S(1)} %broadcast_xor_fusion.groups_ref, f32[2048,2048]{1,0:T(8,128)} %bitcast.20, bf16[512,512]{1,0:T(8,128)(2,1)S(1)} %get-tuple-element.74.refs_0_), custom_call_target="tpu_custom_call" | custom-call | bytes 1024 | tf_op jit(solution)/shard_map/cast_shares/pallas_call | solution.py:80
  65.5 5.9 %update_chunk.5 = (f32[512,2048]{1,0:T(8,128)}, f32[512,2048]{1,0:T(8,128)}, f32[512,2048]{1,0:T(8,128)}, f32[512,128]{1,0:T(8,128)S(1)}, bf16[512,512]{1,0:T(8,128)(2,1)S(1)}) custom-call(s32[1]{0:T(128)} %bitcast.group_ref, f32[2048,2048]{1,0:T(8,128)} %bitcast.21, ...), custom_call_target="tpu_custom_call", output_to_operand_aliasing={{0}: (9, {}), {1}: (10, {}), {2}: (11, {})} | custom-call | bytes 1024 | tf_op jit(solution)/shard_map/update_chunk/pallas_call | solution.py:169
  71.5 3.9 %collective-permute-start.12 = (bf16[512,512]{1,0:T(8,128)(2,1)S(1)}, bf16[512,512]{1,0:T(8,128)(2,1)S(1)}, u32[]{:S(2)}, u32[]{:S(2)}) collective-permute-start(bf16[512,512]{1,0:T(8,128)(2,1)S(1)} %get-tuple-element.84.refs_3_.refs_0_), channel_id=1, source_target_pairs={{0,2},{1,3},{2,6},{3,7},{6,4},{7,5},{4,0},{5,1},{8,10},{9,11},{10,... | collective-permute-start | bytes 1572872 | tf_op jit(solution)/shard_map/ppermute | solution.py:388
  75.4 1.5 collective-permute-start.10
  76.9 1.4 collective-permute-start.11
  78.9 16.4 %collective-permute-done.12.refs_11_.refs_1_ = bf16[512,512]{1,0:T(8,128)(2,1)S(1)} collective-permute-done((bf16[512,512]{1,0:T(8,128)(2,1)S(1)}, bf16[512,512]{1,0:T(8,128)(2,1)S(1)}, u32[]{:S(2)}, u32[]{:S(2)}) %collective-permute-start.12) | collective-permute-done | bytes 524320 | tf_op jit(solution)/shard_map/ppermute | solution.py:388
  95.3 2.5 %cast_shares.7 = (bf16[512,512]{1,0:T(8,128)(2,1)S(1)}, bf16[512,512]{1,0:T(8,128)(2,1)S(1)}, bf16[512,512]{1,0:T(8,128)(2,1)S(1)}) custom-call(s32[3]{0:T(128)S(1)} %broadcast_xor_fusion.groups_ref, f32[2048,2048]{1,0:T(8,128)} %bitcast.22, bf16[512,512]{1,0:T(8,128)(2,1)S(1)} %get-tuple-element.85.refs_0_), custom_call_target="tpu_custom_call" | custom-call | bytes 1024 | tf_op jit(solution)/shard_map/cast_shares/pallas_call | solution.py:80
  97.8 1.2 collective-permute-done.13.refs_12_.refs_2_
  99.6 5.9 %update_chunk.6 = (f32[512,2048]{1,0:T(8,128)}, f32[512,2048]{1,0:T(8,128)}, f32[512,2048]{1,0:T(8,128)}, f32[512,128]{1,0:T(8,128)S(1)}, bf16[512,512]{1,0:T(8,128)(2,1)S(1)}) custom-call(s32[1]{0:T(128)} %bitcast.group_ref, f32[2048,2048]{1,0:T(8,128)} %bitcast.23, ...), custom_call_target="tpu_custom_call", output_to_operand_aliasing={{0}: (9, {}), {1}: (10, {}), {2}: (11, {})} | custom-call | bytes 1024 | tf_op jit(solution)/shard_map/update_chunk/pallas_call | solution.py:169
  106.1 2.7 %collective-permute-done.14.refs_4_.refs_3_ = bf16[512,512]{1,0:T(8,128)(2,1)S(1)} collective-permute-done((bf16[512,512]{1,0:T(8,128)(2,1)S(1)}, bf16[512,512]{1,0:T(8,128)(2,1)S(1)}, u32[]{:S(2)}, u32[]{:S(2)}) %collective-permute-start.14) | collective-permute-done | bytes 524320 | tf_op jit(solution)/shard_map/ppermute | solution.py:388
  108.8 1.8 collective-permute-start.16
  110.6 1.4 collective-permute-start.17
  112.3 7.3 %collective-permute-done.18.refs_5_.refs_11_.refs_1_ = bf16[512,512]{1,0:T(8,128)(2,1)S(1)} collective-permute-done((bf16[512,512]{1,0:T(8,128)(2,1)S(1)}, bf16[512,512]{1,0:T(8,128)(2,1)S(1)}, u32[]{:S(2)}, u32[]{:S(2)}) %collective-permute-start.18) | collective-permute-done | bytes 524320 | tf_op jit(solution)/shard_map/ppermute | solution.py:388
  119.6 2.2 %pick_rows.4 = (bf16[4,256,512]{2,1,0:T(8,128)(2,1)S(1)}, bf16[4,256,512]{2,1,0:T(8,128)(2,1)S(1)}) custom-call(bf16[512,512]{1,0:T(8,128)(2,1)S(1)} %bitcast.11, bf16[512,512]{1,0:T(8,128)(2,1)S(1)} %get-tuple-element.73.refs_3_.refs_0_, bf16[512,512]{1,0:T(8,128)(2,1)S(1)} %collective-permute-done.6.refs_11_.refs_1_, ...), custom_call_target="tpu_custom_call" | custom-call | bytes 1024 | tf_op jit(solution)/shard_map/pick_rows/pallas_call | solution.py:263
  121.8 2.8 %pick_rows.5 = (bf16[4,256,512]{2,1,0:T(8,128)(2,1)S(1)}, bf16[4,256,512]{2,1,0:T(8,128)(2,1)}) custom-call(bf16[512,512]{1,0:T(8,128)(2,1)S(1)} %bitcast.12, bf16[512,512]{1,0:T(8,128)(2,1)S(1)} %get-tuple-element.84.refs_3_.refs_0_, bf16[512,512]{1,0:T(8,128)(2,1)S(1)} %collective-permute-done.12.refs_11_.refs_1_, ...), custom_call_target="tpu_custom_call" | custom-call | bytes 1024 | tf_op jit(solution)/shard_map/pick_rows/pallas_call | solution.py:263
  124.6 6.0 %collective-permute-done.16.refs_1_ = bf16[512,512]{1,0:T(8,128)(2,1)S(1)} collective-permute-done((bf16[512,512]{1,0:T(8,128)(2,1)S(1)}, bf16[512,512]{1,0:T(8,128)(2,1)S(1)}, u32[]{:S(2)}, u32[]{:S(2)}) %collective-permute-start.16) | collective-permute-done | bytes 524320 | tf_op jit(solution)/shard_map/ppermute | solution.py:379
  130.6 7.3 %collective-permute-start.20 = (bf16[512,512]{1,0:T(8,128)(2,1)S(1)}, bf16[512,512]{1,0:T(8,128)(2,1)S(1)}, u32[]{:S(2)}, u32[]{:S(2)}) collective-permute-start(bf16[512,512]{1,0:T(8,128)(2,1)S(1)} %collective-permute-done.18.refs_5_.refs_11_.refs_1_), channel_id=1, source_target_pairs={{0,2},{1,3},{2,6},{3,7},{6,4},{7,5},{4,0},{5,1},{8,10},{9,11},{10,... | collective-permute-start | bytes 1572872 | tf_op jit(solution)/shard_map/ppermute | solution.py:388
  137.9 5.8 %update_chunk.7 = (f32[512,2048]{1,0:T(8,128)}, f32[512,2048]{1,0:T(8,128)}, f32[512,2048]{1,0:T(8,128)}, f32[512,128]{1,0:T(8,128)}, bf16[528,512]{1,0:T(8,128)(2,1)S(1)}, /*index=5*/f32[8,512]{1,0:T(8,128)S(1)}) custom-call(s32[1]{0:T(128)} %bitcast.group_ref, f32[2048,2048]{1,0:T(8,128)} %bitcast.24, ...), custom_call_target="tpu_custom_call", output_to_operand_aliasing={{0}: (9, {}), {1}: (10, {}), {2}: (11, {})} | custom-call | bytes 1024 | tf_op jit(solution)/shard_map/update_chunk/pallas_call | solution.py:169
  143.8 3.4 %collective-permute-start.22 = (bf16[528,512]{1,0:T(8,128)(2,1)S(1)}, bf16[528,512]{1,0:T(8,128)(2,1)S(1)}, u32[]{:S(2)}, u32[]{:S(2)}) collective-permute-start(bf16[528,512]{1,0:T(8,128)(2,1)S(1)} %get-tuple-element.109.refs_1_.refs_0_), channel_id=1, source_target_pairs={{0,2},{1,3},{2,6},{3,7},{6,4},{7,5},{4,0},{5,1},{8,10},{9,11},{10,... | collective-permute-start | bytes 1622024 | tf_op jit(solution)/shard_map/ppermute | solution.py:388
  147.2 3.0 %collective-permute-done.20.refs_2_.refs_3_ = bf16[512,512]{1,0:T(8,128)(2,1)S(1)} collective-permute-done((bf16[512,512]{1,0:T(8,128)(2,1)S(1)}, bf16[512,512]{1,0:T(8,128)(2,1)S(1)}, u32[]{:S(2)}, u32[]{:S(2)}) %collective-permute-start.20) | collective-permute-done | bytes 524320 | tf_op jit(solution)/shard_map/ppermute | solution.py:388
  150.2 17.8 %collective-permute-start.21 = (f32[8,512]{1,0:T(8,128)S(1)}, f32[8,512]{1,0:T(8,128)S(1)}, u32[]{:S(2)}, u32[]{:S(2)}) collective-permute-start(f32[8,512]{1,0:T(8,128)S(1)} %pass_after.7.refs_4_.high_ref), channel_id=1, source_target_pairs={{0,6},{1,7},{2,4},{3,5},{6,0},{7,1},{4,2},{5,3},{8,14},{9,15},{10,... | collective-permute-start | bytes 49160 | tf_op jit(solution)/shard_map/ppermute | solution.py:388
  168.0 2.2 %pick_rows.6 = (bf16[4,256,512]{2,1,0:T(8,128)(2,1)S(1)}, bf16[4,256,512]{2,1,0:T(8,128)(2,1)S(1)}) custom-call(bf16[512,512]{1,0:T(8,128)(2,1)S(1)} %bitcast.13, bf16[512,512]{1,0:T(8,128)(2,1)S(1)} %get-tuple-element.95.refs_3_.refs_0_, bf16[512,512]{1,0:T(8,128)(2,1)S(1)} %collective-permute-done.18.refs_5_.refs_11_.refs_1_, ...), custom_call_target="tpu_custom_call" | custom-call | bytes 1024 | tf_op jit(solution)/shard_map/pick_rows/pallas_call | solution.py:263
  170.2 6.2 %collective-permute-done.21.across_ref = f32[8,512]{1,0:T(8,128)S(1)} collective-permute-done((f32[8,512]{1,0:T(8,128)S(1)}, f32[8,512]{1,0:T(8,128)S(1)}, u32[]{:S(2)}, u32[]{:S(2)}) %collective-permute-start.21) | collective-permute-done | bytes 16416 | tf_op jit(solution)/shard_map/ppermute | solution.py:388
  176.8 2.8 %collective-permute-start.26 = (bf16[512,256]{1,0:T(8,128)(2,1)S(1)}, bf16[512,256]{1,0:T(8,128)(2,1)S(1)}, u32[]{:S(2)}, u32[]{:S(2)}) collective-permute-start(bf16[512,256]{1,0:T(8,128)(2,1)S(1)} %get-tuple-element.112.refs_3_), channel_id=1, source_target_pairs={{0,4},{1,5},{2,0},{3,1},{6,2},{7,3},{4,6},{5,7},{8,12},{9,13},{10,... | collective-permute-start | bytes 786440 | tf_op jit(solution)/shard_map/ppermute | solution.py:388
  179.6 1.2 collective-permute-done.24.refs_1_
  180.9 0.7 slot_scales.1
  181.7 0.7 copy-done
  182.4 2.4 %store_rows.4 = (bf16[256,16384]{1,0:T(8,128)(2,1)}, f32[8,128]{1,0:T(8,128)S(1)}) custom-call(s32[8]{0:T(128)S(1)} %reshape.103.refs_2_.place_ref, f32[256,1]{1,0:T(8,128)S(1)} %get-tuple-element.113.inverse_ref, bf16[4,256,512]{2,1,0:T(8,128)(2,1)S(1)} %get-tuple-element.103.refs_4_.mine_ref, bf16[4,256,512]{2,1,0:T(8,128)(2,1)S(1)} %collective-permute-done.28.other_ref, ...), custom_call_target="tpu_custom_call" | custom-call | bytes 1024 | tf_op jit(solution)/shard_map/store_rows/pallas_call | solution.py:297
  184.8 2.4 %store_rows.5 = (bf16[256,16384]{1,0:T(8,128)(2,1)}, f32[8,128]{1,0:T(8,128)S(1)}) custom-call(s32[8]{0:T(128)S(1)} %reshape.103.refs_2_.place_ref, f32[256,1]{1,0:T(8,128)S(1)} %get-tuple-element.113.inverse_ref, bf16[4,256,512]{2,1,0:T(8,128)(2,1)S(1)} %get-tuple-element.104.refs_10_.mine_ref, ...), custom_call_target="tpu_custom_call", output_to_operand_aliasing={{0}: (4, {})} | custom-call | bytes 1024 | tf_op jit(solution)/shard_map/store_rows/pallas_call | solution.py:297
  187.2 3.5 %collective-permute-done.26.refs_4_ = bf16[512,256]{1,0:T(8,128)(2,1)S(1)} collective-permute-done((bf16[512,256]{1,0:T(8,128)(2,1)S(1)}, bf16[512,256]{1,0:T(8,128)(2,1)S(1)}, u32[]{:S(2)}, u32[]{:S(2)}) %collective-permute-start.26) | collective-permute-done | bytes 262176 | tf_op jit(solution)/shard_map/ppermute | solution.py:388
  190.6 2.2 %pick_rows.7 = (bf16[4,256,512]{2,1,0:T(8,128)(2,1)S(1)}, bf16[4,256,512]{2,1,0:T(8,128)(2,1)S(1)}) custom-call(bf16[512,512]{1,0:T(8,128)(2,1)S(1)} %bitcast.15, bf16[528,512]{1,0:T(8,128)(2,1)S(1)} %get-tuple-element.109.refs_1_.refs_0_, bf16[528,512]{1,0:T(8,128)(2,1)S(1)} %collective-permute-done.22.ahead_ref.refs_1_, ...), custom_call_target="tpu_custom_call" | custom-call | bytes 1024 | tf_op jit(solution)/shard_map/pick_rows/pallas_call | solution.py:263
  192.9 2.4 %store_rows.6 = (bf16[256,16384]{1,0:T(8,128)(2,1)}, f32[8,128]{1,0:T(8,128)S(1)}) custom-call(s32[8]{0:T(128)S(1)} %reshape.103.refs_2_.place_ref, f32[256,1]{1,0:T(8,128)S(1)} %get-tuple-element.113.inverse_ref, bf16[4,256,512]{2,1,0:T(8,128)(2,1)S(1)} %get-tuple-element.110.refs_0_.mine_ref, ...), custom_call_target="tpu_custom_call", output_to_operand_aliasing={{0}: (4, {})} | custom-call | bytes 1024 | tf_op jit(solution)/shard_map/store_rows/pallas_call | solution.py:297
  195.6 3.0 %store_rows.7 = (bf16[256,16384]{1,0:T(8,128)(2,1)}, f32[8,128]{1,0:T(8,128)}) custom-call(s32[8]{0:T(128)S(1)} %reshape.103.refs_2_.place_ref, f32[256,1]{1,0:T(8,128)S(1)} %get-tuple-element.113.inverse_ref, bf16[4,256,512]{2,1,0:T(8,128)(2,1)S(1)} %get-tuple-element.120.refs_1_.mine_ref, ...), custom_call_target="tpu_custom_call", output_to_operand_aliasing={{0}: (4, {})} | custom-call | bytes 1024 | tf_op jit(solution)/shard_map/store_rows/pallas_call | solution.py:297
  (60 shorter events, 5.5 us)
Async XLA Ops:
  1.3 7.1 %copy-start.1 = (s32[4]{0:T(128)S(1)}, s32[4]{0:T(128)}, u32[]{:S(2)}) copy-start(s32[4]{0:T(128)} %constant.64.clone) | copy-start | bytes 52
  1.3 7.8 %copy-start.4 = (s32[4]{0:T(128)S(1)}, s32[4]{0:T(128)}, u32[]{:S(2)}) copy-start(s32[4]{0:T(128)} %constant.65.clone) | copy-start | bytes 52
  1.3 9.2 %copy-start.3 = (s32[512]{0:T(512)S(1)}, s32[512]{0:T(512)}, u32[]{:S(2)}) copy-start(s32[512]{0:T(512)} %param.17) | copy-start | bytes 6148
  1.3 9.5 %copy-start.2 = (s32[512]{0:T(512)S(1)}, s32[512]{0:T(512)}, u32[]{:S(2)}) copy-start(s32[512]{0:T(512)} %param.18) | copy-start | bytes 6148
  3.9 26.2 %collective-permute-start.1 = (bf16[512,512]{1,0:T(8,128)(2,1)S(1)}, bf16[512,512]{1,0:T(8,128)(2,1)S(1)}, u32[]{:S(2)}, u32[]{:S(2)}) collective-permute-start(bf16[512,512]{1,0:T(8,128)(2,1)S(1)} %get-tuple-element.71), channel_id=1, source_target_pairs={{0,16},{8,24},{16,0},{24,8},{1,17},{9,25},{17,1},{25,9},{2,18},{10... | collective-permute-start | bytes 1572872 | tf_op jit(solution)/shard_map/ppermute | solution.py:379
  6.9 23.2 %collective-permute-start.2 = (bf16[512,512]{1,0:T(8,128)(2,1)S(1)}, bf16[512,512]{1,0:T(8,128)(2,1)S(1)}, u32[]{:S(2)}, u32[]{:S(2)}) collective-permute-start(bf16[512,512]{1,0:T(8,128)(2,1)S(1)} %get-tuple-element.72), channel_id=1, source_target_pairs={{0,24},{8,16},{16,8},{24,0},{1,25},{9,17},{17,9},{25,1},{2,26},{10... | collective-permute-start | bytes 1572872 | tf_op jit(solution)/shard_map/ppermute | solution.py:379
  8.3 23.0 %collective-permute-start = (bf16[512,512]{1,0:T(8,128)(2,1)S(1)}, bf16[512,512]{1,0:T(8,128)(2,1)S(1)}, u32[]{:S(2)}, u32[]{:S(2)}) collective-permute-start(bf16[512,512]{1,0:T(8,128)(2,1)S(1)} %get-tuple-element.66.refs_0_), channel_id=1, source_target_pairs={{0,8},{8,0},{16,24},{24,16},{1,9},{9,1},{17,25},{25,17},{2,10},{10... | collective-permute-start | bytes 1572872 | tf_op jit(solution)/shard_map/ppermute | solution.py:379
  37.0 15.3 %collective-permute-start.6 = (bf16[512,512]{1,0:T(8,128)(2,1)S(1)}, bf16[512,512]{1,0:T(8,128)(2,1)S(1)}, u32[]{:S(2)}, u32[]{:S(2)}) collective-permute-start(bf16[512,512]{1,0:T(8,128)(2,1)S(1)} %get-tuple-element.73.refs_3_.refs_0_), channel_id=1, source_target_pairs={{0,2},{1,3},{2,6},{3,7},{6,4},{7,5},{4,0},{5,1},{8,10},{9,11},{10,... | collective-permute-start | bytes 1572872 | tf_op jit(solution)/shard_map/ppermute | solution.py:388
  38.7 26.8 %collective-permute-start.4 = (bf16[512,512]{1,0:T(8,128)(2,1)S(1)}, bf16[512,512]{1,0:T(8,128)(2,1)S(1)}, u32[]{:S(2)}, u32[]{:S(2)}) collective-permute-start(bf16[512,512]{1,0:T(8,128)(2,1)S(1)} %get-tuple-element.78), channel_id=1, source_target_pairs={{0,16},{8,24},{16,0},{24,8},{1,17},{9,25},{17,1},{25,9},{2,18},{10... | collective-permute-start | bytes 1572872 | tf_op jit(solution)/shard_map/ppermute | solution.py:379
  40.2 25.2 %collective-permute-start.5 = (bf16[512,512]{1,0:T(8,128)(2,1)S(1)}, bf16[512,512]{1,0:T(8,128)(2,1)S(1)}, u32[]{:S(2)}, u32[]{:S(2)}) collective-permute-start(bf16[512,512]{1,0:T(8,128)(2,1)S(1)} %get-tuple-element.79), channel_id=1, source_target_pairs={{0,24},{8,16},{16,8},{24,0},{1,25},{9,17},{17,9},{25,1},{2,26},{10... | collective-permute-start | bytes 1572872 | tf_op jit(solution)/shard_map/ppermute | solution.py:379
  41.7 23.8 %collective-permute-start.3 = (bf16[512,512]{1,0:T(8,128)(2,1)S(1)}, bf16[512,512]{1,0:T(8,128)(2,1)S(1)}, u32[]{:S(2)}, u32[]{:S(2)}) collective-permute-start(bf16[512,512]{1,0:T(8,128)(2,1)S(1)} %get-tuple-element.74.refs_0_), channel_id=1, source_target_pairs={{0,8},{8,0},{16,24},{24,16},{1,9},{9,1},{17,25},{25,17},{2,10},{10... | collective-permute-start | bytes 1572872 | tf_op jit(solution)/shard_map/ppermute | solution.py:379
  42.2 23.3 %collective-permute-start.7 = (bf16[512,512]{1,0:T(8,128)(2,1)S(1)}, bf16[512,512]{1,0:T(8,128)(2,1)S(1)}, u32[]{:S(2)}, u32[]{:S(2)}) collective-permute-start(bf16[512,512]{1,0:T(8,128)(2,1)S(1)} %get-tuple-element.73.refs_3_.refs_0_), channel_id=1, source_target_pairs={{0,4},{1,5},{2,0},{3,1},{6,2},{7,3},{4,6},{5,7},{8,12},{9,13},{10,... | collective-permute-start | bytes 1572872 | tf_op jit(solution)/shard_map/ppermute | solution.py:388
  52.2 23.2 %collective-permute-start.8 = (bf16[512,512]{1,0:T(8,128)(2,1)S(1)}, bf16[512,512]{1,0:T(8,128)(2,1)S(1)}, u32[]{:S(2)}, u32[]{:S(2)}) collective-permute-start(bf16[512,512]{1,0:T(8,128)(2,1)S(1)} %collective-permute-done.6.refs_11_.refs_1_), channel_id=1, source_target_pairs={{0,2},{1,3},{2,6},{3,7},{6,4},{7,5},{4,0},{5,1},{8,10},{9,11},{10,... | collective-permute-start | bytes 1572872 | tf_op jit(solution)/shard_map/ppermute | solution.py:388
  71.5 23.8 %collective-permute-start.12 = (bf16[512,512]{1,0:T(8,128)(2,1)S(1)}, bf16[512,512]{1,0:T(8,128)(2,1)S(1)}, u32[]{:S(2)}, u32[]{:S(2)}) collective-permute-start(bf16[512,512]{1,0:T(8,128)(2,1)S(1)} %get-tuple-element.84.refs_3_.refs_0_), channel_id=1, source_target_pairs={{0,2},{1,3},{2,6},{3,7},{6,4},{7,5},{4,0},{5,1},{8,10},{9,11},{10,... | collective-permute-start | bytes 1572872 | tf_op jit(solution)/shard_map/ppermute | solution.py:388
  75.4 23.6 %collective-permute-start.13 = (bf16[512,512]{1,0:T(8,128)(2,1)S(1)}, bf16[512,512]{1,0:T(8,128)(2,1)S(1)}, u32[]{:S(2)}, u32[]{:S(2)}) collective-permute-start(bf16[512,512]{1,0:T(8,128)(2,1)S(1)} %get-tuple-element.84.refs_3_.refs_0_), channel_id=1, source_target_pairs={{0,4},{1,5},{2,0},{3,1},{6,2},{7,3},{4,6},{5,7},{8,12},{9,13},{10,... | collective-permute-start | bytes 1572872 | tf_op jit(solution)/shard_map/ppermute | solution.py:388
  75.4 23.6 %collective-permute-start.10 = (bf16[512,512]{1,0:T(8,128)(2,1)S(1)}, bf16[512,512]{1,0:T(8,128)(2,1)S(1)}, u32[]{:S(2)}, u32[]{:S(2)}) collective-permute-start(bf16[512,512]{1,0:T(8,128)(2,1)S(1)} %get-tuple-element.89), channel_id=1, source_target_pairs={{0,16},{8,24},{16,0},{24,8},{1,17},{9,25},{17,1},{25,9},{2,18},{10... | collective-permute-start | bytes 1572872 | tf_op jit(solution)/shard_map/ppermute | solution.py:379
  76.9 22.1 %collective-permute-start.11 = (bf16[512,512]{1,0:T(8,128)(2,1)S(1)}, bf16[512,512]{1,0:T(8,128)(2,1)S(1)}, u32[]{:S(2)}, u32[]{:S(2)}) collective-permute-start(bf16[512,512]{1,0:T(8,128)(2,1)S(1)} %get-tuple-element.90), channel_id=1, source_target_pairs={{0,24},{8,16},{16,8},{24,0},{1,25},{9,17},{17,9},{25,1},{2,26},{10... | collective-permute-start | bytes 1572872 | tf_op jit(solution)/shard_map/ppermute | solution.py:379
  78.3 21.3 %collective-permute-start.9 = (bf16[512,512]{1,0:T(8,128)(2,1)S(1)}, bf16[512,512]{1,0:T(8,128)(2,1)S(1)}, u32[]{:S(2)}, u32[]{:S(2)}) collective-permute-start(bf16[512,512]{1,0:T(8,128)(2,1)S(1)} %get-tuple-element.85.refs_0_), channel_id=1, source_target_pairs={{0,8},{8,0},{16,24},{24,16},{1,9},{9,1},{17,25},{25,17},{2,10},{10... | collective-permute-start | bytes 1572872 | tf_op jit(solution)/shard_map/ppermute | solution.py:379
  95.3 13.5 %collective-permute-start.14 = (bf16[512,512]{1,0:T(8,128)(2,1)S(1)}, bf16[512,512]{1,0:T(8,128)(2,1)S(1)}, u32[]{:S(2)}, u32[]{:S(2)}) collective-permute-start(bf16[512,512]{1,0:T(8,128)(2,1)S(1)} %collective-permute-done.12.refs_11_.refs_1_), channel_id=1, source_target_pairs={{0,2},{1,3},{2,6},{3,7},{6,4},{7,5},{4,0},{5,1},{8,10},{9,11},{10,... | collective-permute-start | bytes 1572872 | tf_op jit(solution)/shard_map/ppermute | solution.py:388
  105.6 14.0 %collective-permute-start.18 = (bf16[512,512]{1,0:T(8,128)(2,1)S(1)}, bf16[512,512]{1,0:T(8,128)(2,1)S(1)}, u32[]{:S(2)}, u32[]{:S(2)}) collective-permute-start(bf16[512,512]{1,0:T(8,128)(2,1)S(1)} %get-tuple-element.95.refs_3_.refs_0_), channel_id=1, source_target_pairs={{0,2},{1,3},{2,6},{3,7},{6,4},{7,5},{4,0},{5,1},{8,10},{9,11},{10,... | collective-permute-start | bytes 1572872 | tf_op jit(solution)/shard_map/ppermute | solution.py:388
  108.8 21.8 %collective-permute-start.16 = (bf16[512,512]{1,0:T(8,128)(2,1)S(1)}, bf16[512,512]{1,0:T(8,128)(2,1)S(1)}, u32[]{:S(2)}, u32[]{:S(2)}) collective-permute-start(bf16[512,512]{1,0:T(8,128)(2,1)S(1)} %get-tuple-element.97), channel_id=1, source_target_pairs={{0,16},{8,24},{16,0},{24,8},{1,17},{9,25},{17,1},{25,9},{2,18},{10... | collective-permute-start | bytes 1572872 | tf_op jit(solution)/shard_map/ppermute | solution.py:379
  110.6 20.0 %collective-permute-start.17 = (bf16[512,512]{1,0:T(8,128)(2,1)S(1)}, bf16[512,512]{1,0:T(8,128)(2,1)S(1)}, u32[]{:S(2)}, u32[]{:S(2)}) collective-permute-start(bf16[512,512]{1,0:T(8,128)(2,1)S(1)} %get-tuple-element.98), channel_id=1, source_target_pairs={{0,24},{8,16},{16,8},{24,0},{1,25},{9,17},{17,9},{25,1},{2,26},{10... | collective-permute-start | bytes 1572872 | tf_op jit(solution)/shard_map/ppermute | solution.py:379
  112.0 25.9 %collective-permute-start.15 = (bf16[512,512]{1,0:T(8,128)(2,1)S(1)}, bf16[512,512]{1,0:T(8,128)(2,1)S(1)}, u32[]{:S(2)}, u32[]{:S(2)}) collective-permute-start(bf16[512,512]{1,0:T(8,128)(2,1)S(1)} %get-tuple-element.96.refs_4_), channel_id=1, source_target_pairs={{0,8},{8,0},{16,24},{24,16},{1,9},{9,1},{17,25},{25,17},{2,10},{10... | collective-permute-start | bytes 1572872 | tf_op jit(solution)/shard_map/ppermute | solution.py:379
  112.3 25.6 %collective-permute-start.19 = (bf16[512,512]{1,0:T(8,128)(2,1)S(1)}, bf16[512,512]{1,0:T(8,128)(2,1)S(1)}, u32[]{:S(2)}, u32[]{:S(2)}) collective-permute-start(bf16[512,512]{1,0:T(8,128)(2,1)S(1)} %get-tuple-element.95.refs_3_.refs_0_), channel_id=1, source_target_pairs={{0,4},{1,5},{2,0},{3,1},{6,2},{7,3},{4,6},{5,7},{8,12},{9,13},{10,... | collective-permute-start | bytes 1572872 | tf_op jit(solution)/shard_map/ppermute | solution.py:388
  121.7 60.0 %collective-permute-start.28 = (bf16[4,256,512]{2,1,0:T(8,128)(2,1)S(1)}, bf16[4,256,512]{2,1,0:T(8,128)(2,1)S(1)}, u32[]{:S(2)}, u32[]{:S(2)}) collective-permute-start(bf16[4,256,512]{2,1,0:T(8,128)(2,1)S(1)} %get-tuple-element.115), channel_id=1, source_target_pairs={{0,1},{1,0},{2,3},{3,2},{4,5},{5,4},{6,7},{7,6},{8,9},{9,8},{10,11... | collective-permute-start | bytes 3145736 | tf_op jit(solution)/shard_map/ppermute | solution.py:391
  130.6 54.2 %collective-permute-start.27 = (bf16[4,256,512]{2,1,0:T(8,128)(2,1)}, bf16[4,256,512]{2,1,0:T(8,128)(2,1)S(1)}, u32[]{:S(2)}, u32[]{:S(2)}) collective-permute-start(bf16[4,256,512]{2,1,0:T(8,128)(2,1)} %get-tuple-element.114), channel_id=1, source_target_pairs={{0,1},{1,0},{2,3},{3,2},{4,5},{5,4},{6,7},{7,6},{8,9},{9,8},{10,11... | collective-permute-start | bytes 3145736 | tf_op jit(solution)/shard_map/ppermute | solution.py:391
  130.6 19.6 %collective-permute-start.20 = (bf16[512,512]{1,0:T(8,128)(2,1)S(1)}, bf16[512,512]{1,0:T(8,128)(2,1)S(1)}, u32[]{:S(2)}, u32[]{:S(2)}) collective-permute-start(bf16[512,512]{1,0:T(8,128)(2,1)S(1)} %collective-permute-done.18.refs_5_.refs_11_.refs_1_), channel_id=1, source_target_pairs={{0,2},{1,3},{2,6},{3,7},{6,4},{7,5},{4,0},{5,1},{8,10},{9,11},{10,... | collective-permute-start | bytes 1572872 | tf_op jit(solution)/shard_map/ppermute | solution.py:388
  143.7 32.7 %collective-permute-start.23 = (bf16[528,512]{1,0:T(8,128)(2,1)S(1)}, bf16[528,512]{1,0:T(8,128)(2,1)S(1)}, u32[]{:S(2)}, u32[]{:S(2)}) collective-permute-start(bf16[528,512]{1,0:T(8,128)(2,1)S(1)} %get-tuple-element.109.refs_1_.refs_0_), channel_id=1, source_target_pairs={{0,4},{1,5},{2,0},{3,1},{6,2},{7,3},{4,6},{5,7},{8,12},{9,13},{10,... | collective-permute-start | bytes 1622024 | tf_op jit(solution)/shard_map/ppermute | solution.py:388
  143.8 32.7 %collective-permute-start.22 = (bf16[528,512]{1,0:T(8,128)(2,1)S(1)}, bf16[528,512]{1,0:T(8,128)(2,1)S(1)}, u32[]{:S(2)}, u32[]{:S(2)}) collective-permute-start(bf16[528,512]{1,0:T(8,128)(2,1)S(1)} %get-tuple-element.109.refs_1_.refs_0_), channel_id=1, source_target_pairs={{0,2},{1,3},{2,6},{3,7},{6,4},{7,5},{4,0},{5,1},{8,10},{9,11},{10,... | collective-permute-start | bytes 1622024 | tf_op jit(solution)/shard_map/ppermute | solution.py:388
  150.2 26.2 %collective-permute-start.21 = (f32[8,512]{1,0:T(8,128)S(1)}, f32[8,512]{1,0:T(8,128)S(1)}, u32[]{:S(2)}, u32[]{:S(2)}) collective-permute-start(f32[8,512]{1,0:T(8,128)S(1)} %pass_after.7.refs_4_.high_ref), channel_id=1, source_target_pairs={{0,6},{1,7},{2,4},{3,5},{6,0},{7,1},{4,2},{5,3},{8,14},{9,15},{10,... | collective-permute-start | bytes 49160 | tf_op jit(solution)/shard_map/ppermute | solution.py:388
  176.6 10.5 %collective-permute-start.25 = (bf16[512,256]{1,0:T(8,128)(2,1)S(1)}, bf16[512,256]{1,0:T(8,128)(2,1)S(1)}, u32[]{:S(2)}, u32[]{:S(2)}) collective-permute-start(bf16[512,256]{1,0:T(8,128)(2,1)S(1)} %get-tuple-element.111.refs_2_), channel_id=1, source_target_pairs={{0,2},{1,3},{2,6},{3,7},{6,4},{7,5},{4,0},{5,1},{8,10},{9,11},{10,... | collective-permute-start | bytes 786440 | tf_op jit(solution)/shard_map/ppermute | solution.py:388
  176.8 13.8 %collective-permute-start.26 = (bf16[512,256]{1,0:T(8,128)(2,1)S(1)}, bf16[512,256]{1,0:T(8,128)(2,1)S(1)}, u32[]{:S(2)}, u32[]{:S(2)}) collective-permute-start(bf16[512,256]{1,0:T(8,128)(2,1)S(1)} %get-tuple-element.112.refs_3_), channel_id=1, source_target_pairs={{0,4},{1,5},{2,0},{3,1},{6,2},{7,3},{4,6},{5,7},{8,12},{9,13},{10,... | collective-permute-start | bytes 786440 | tf_op jit(solution)/shard_map/ppermute | solution.py:388
  179.6 1.2 collective-permute-start.24
  180.8 12.1 %collective-permute-start.30 = (bf16[4,256,512]{2,1,0:T(8,128)(2,1)S(1)}, bf16[4,256,512]{2,1,0:T(8,128)(2,1)S(1)}, u32[]{:S(2)}, u32[]{:S(2)}) collective-permute-start(bf16[4,256,512]{2,1,0:T(8,128)(2,1)S(1)} %get-tuple-element.122), channel_id=1, source_target_pairs={{0,1},{1,0},{2,3},{3,2},{4,5},{5,4},{6,7},{7,6},{8,9},{9,8},{10,11... | collective-permute-start | bytes 3145736 | tf_op jit(solution)/shard_map/ppermute | solution.py:391
  181.7 0.7 copy-start
  192.8 2.7 %collective-permute-start.29 = (bf16[4,256,512]{2,1,0:T(8,128)(2,1)S(1)}, bf16[4,256,512]{2,1,0:T(8,128)(2,1)S(1)}, u32[]{:S(2)}, u32[]{:S(2)}) collective-permute-start(bf16[4,256,512]{2,1,0:T(8,128)(2,1)S(1)} %get-tuple-element.121), channel_id=1, source_target_pairs={{0,1},{1,0},{2,3},{3,2},{4,5},{5,4},{6,7},{7,6},{8,9},{9,8},{10,11... | collective-permute-start | bytes 3145736 | tf_op jit(solution)/shard_map/ppermute | solution.py:391

commit v3 on v1

--- a/solution.py
+++ b/solution.py
@@ -57,14 +57,15 @@
     return pl.ds(pl.multiple_of(groups_ref[j] * rows + tile * height, 16), height)
 
 
-def cast_kernel(start, groups_ref, grads_ref, *refs):
+def cast_kernel(start, grads_ref, *refs):
     outs, (held, packed, in_sems, out_sems) = refs[-7:-4], refs[-4:]
     size = held.shape[2]
     height = held.shape[1]
     rows = height * CAST_TILES
     where = [(j, t) for t in range(CAST_TILES) for j in range(3)]
     columns = pl.ds(start, size)
-    sources = [grads_ref.at[group_rows(groups_ref, j, t, rows, CAST_TILES), columns] for j, t in where]
+    groups = [lax.axis_index("rep") ^ mask for mask in (1, 2, 3)]
+    sources = [grads_ref.at[group_rows(groups, j, t, rows, CAST_TILES), columns] for j, t in where]
     arriving = start_copies([(source, held.at[i]) for i, source in enumerate(sources)], in_sems)
     leaving = []
     for i, (j, t) in enumerate(where):
@@ -74,12 +75,12 @@
     wait_copies(leaving)
 
 
-def cast_shares(grads, groups, after, rows, start, size):
+def cast_shares(grads, after, rows, start, size):
     tiles = 3 * CAST_TILES
     height = rows // CAST_TILES
     return pl.pallas_call(
         functools.partial(cast_kernel, start),
-        in_specs=[SMEM, ANY] + [ANY] * len(after),
+        in_specs=[ANY] * (1 + len(after)),
         out_specs=[ANY] * 3,
         out_shape=[jax.ShapeDtypeStruct((rows, size), jnp.bfloat16)] * 3,
         scratch_shapes=[
@@ -91,10 +92,10 @@
         compiler_params=params(),
         cost_estimate=cost(3 * rows * size * 6),
         name="cast_shares",
-    )(groups, grads, *after)
-
-
-UPDATE_TILES = 4
+    )(grads, *after)
+
+
+UPDATE_TILES = 8
 PEAK_ROWS = 16
 
 
@@ -412,7 +413,7 @@
         if kind == "cast":
             if k == 1:
                 after = after + [pick_both, place]
-            shares = cast_shares(grads, groups(1, 2, 3), after, rows, starts[k], CHUNKS[k])
+            shares = cast_shares(grads, after, rows, starts[k], CHUNKS[k])
             after = [shares[0]]
         elif kind == "sum":
             if k > 0:

time: 196 us -> 196 us (level)
  starting transfers between devices: 58.4 us -> 62.3 us
  waiting for transfers between devices: 78.5 us -> 75.4 us
    ppermute x14, starting transfers between devices: 42.5 us -> 46.2 us  [turn_by(): return lax.ppermute(value, 'wide', pairs)]
    pallas_call x4, Pallas kernels: 10.2 us -> 8.03 us  [cast_shares(): pl.pallas_call(functools.partial(cast_kernel, start), in_specs=[ANY] * (1...]
    ppermute x14, waiting for transfers between devices: 44.8 us -> 42.7 us  [turn_by(): return lax.ppermute(value, 'wide', pairs)]
where the time goes in v3:
time: 196 us; the launch traced here: 195 us
  waiting for transfers between devices  75.4 us (38%)
  starting transfers between devices  62.3 us (32%)
  Pallas kernels  53.5 us (27%)
    ppermute x14, starting transfers between devices, turn_by(): return lax.ppermute(value, 'wide', pairs)  46.2 us
    ppermute x14, waiting for transfers between devices, turn_by(): return lax.ppermute(value, 'wide', pairs)  42.7 us
    ppermute x12, waiting for transfers between devices, swap(): return lax.ppermute(value, 'rep', [(i, i ^ mask) for i in range(n_rep)])  31.2 us
    pallas_call x4, Pallas kernels, update_chunk(): pl.pallas_call(functools.partial(update_kernel, start, first_chunk, last_...  25.2 us
    ppermute x12, starting transfers between devices, swap(): return lax.ppermute(value, 'rep', [(i, i ^ mask) for i in range(n_rep)])  15.2 us
    pallas_call x4, Pallas kernels, store_rows(): pl.pallas_call(functools.partial(store_kernel, start, width), in_specs=[S...  10.1 us
    pallas_call x4, Pallas kernels, pick_rows(): pl.pallas_call(functools.partial(pick_kernel, n_sources), in_specs=[VMEM]...  9.28 us
    pallas_call x4, Pallas kernels, cast_shares(): pl.pallas_call(functools.partial(cast_kernel, start), in_specs=[ANY] * (1...  8.03 us
  transfers between devices with their start and end apart: 31, of which 13 were waited for; matrix products, arithmetic and copies ran while one was open for 1% of the time, Pallas kernels for 22%

profile of v3, /device:TPU:0, one launch (start us, length us, event | category | flops | bytes accessed | tf_op | source)
XLA Modules:
  0.0 195.4 jit_solution(573289991684729109)
XLA Ops:
  0.7 2.0 %cast_shares.4 = (bf16[512,512]{1,0:T(8,128)(2,1)S(1)}, bf16[512,512]{1,0:T(8,128)(2,1)S(1)}, bf16[512,512]{1,0:T(8,128)(2,1)S(1)}) custom-call(f32[2048,2048]{1,0:T(8,128)} %bitcast.17), custom_call_target="tpu_custom_call" | custom-call | bytes 1024 | tf_op jit(solution)/shard_map/cast_shares/pallas_call | solution.py:81
  2.7 3.0 %collective-permute-start.1 = (bf16[512,512]{1,0:T(8,128)(2,1)S(1)}, bf16[512,512]{1,0:T(8,128)(2,1)S(1)}, u32[]{:S(2)}, u32[]{:S(2)}) collective-permute-start(bf16[512,512]{1,0:T(8,128)(2,1)S(1)} %get-tuple-element.71), channel_id=1, source_target_pairs={{0,16},{8,24},{16,0},{24,8},{1,17},{9,25},{17,1},{25,9},{2,18},{10... | collective-permute-start | bytes 1572872 | tf_op jit(solution)/shard_map/ppermute | solution.py:380
  5.7 1.4 collective-permute-start.2
  7.9 0.7 compare_select_fusion
  9.8 2.0 %cast_shares.5 = (bf16[512,512]{1,0:T(8,128)(2,1)S(1)}, bf16[512,512]{1,0:T(8,128)(2,1)S(1)}, bf16[512,512]{1,0:T(8,128)(2,1)S(1)}) custom-call(f32[2048,2048]{1,0:T(8,128)} %bitcast.18, bf16[512,512]{1,0:T(8,128)(2,1)S(1)} %get-tuple-element.66.refs_0_, bf16[512,512]{1,0:T(8,128)(2,1)S(1)} %bitcast.10, s32[8]{0:T(128)S(1)} %reshape.103.refs_2_.refs_0_), custom_call_target="tpu_custom_call" | custom-call | bytes 1024 | tf_op jit(solution)/shard_map/cast_shares/pallas_call | solution.py:81
  11.8 17.1 %collective-permute-done.1.refs_1_ = bf16[512,512]{1,0:T(8,128)(2,1)S(1)} collective-permute-done((bf16[512,512]{1,0:T(8,128)(2,1)S(1)}, bf16[512,512]{1,0:T(8,128)(2,1)S(1)}, u32[]{:S(2)}, u32[]{:S(2)}) %collective-permute-start.1) | collective-permute-done | bytes 524320 | tf_op jit(solution)/shard_map/ppermute | solution.py:380
  28.9 1.3 collective-permute-done.refs_0_
  30.2 6.1 %update_chunk.4 = (f32[512,2048]{1,0:T(8,128)}, f32[512,2048]{1,0:T(8,128)}, f32[512,2048]{1,0:T(8,128)}, f32[512,128]{1,0:T(8,128)S(1)}, bf16[512,512]{1,0:T(8,128)(2,1)S(1)}) custom-call(s32[1]{0:T(128)} %bitcast.group_ref, f32[2048,2048]{1,0:T(8,128)} %bitcast.19, bf16[512,512]{1,0:T(8,128)(2,1)S(1)} %collective-permute-done.refs_0_, ...), custom_call_target="tpu_custom_call" | custom-call | bytes 1024 | tf_op jit(solution)/shard_map/update_chunk/pallas_call | solution.py:170
  36.3 1.8 collective-permute-start.6
  38.1 1.5 collective-permute-start.4
  39.6 1.4 collective-permute-start.5
  41.5 1.2 collective-permute-start.7
  42.7 8.8 %collective-permute-done.6.refs_11_.refs_1_ = bf16[512,512]{1,0:T(8,128)(2,1)S(1)} collective-permute-done((bf16[512,512]{1,0:T(8,128)(2,1)S(1)}, bf16[512,512]{1,0:T(8,128)(2,1)S(1)}, u32[]{:S(2)}, u32[]{:S(2)}) %collective-permute-start.6) | collective-permute-done | bytes 524320 | tf_op jit(solution)/shard_map/ppermute | solution.py:389
  51.5 10.7 %collective-permute-start.8 = (bf16[512,512]{1,0:T(8,128)(2,1)S(1)}, bf16[512,512]{1,0:T(8,128)(2,1)S(1)}, u32[]{:S(2)}, u32[]{:S(2)}) collective-permute-start(bf16[512,512]{1,0:T(8,128)(2,1)S(1)} %collective-permute-done.6.refs_11_.refs_1_), channel_id=1, source_target_pairs={{0,2},{1,3},{2,6},{3,7},{6,4},{7,5},{4,0},{5,1},{8,10},{9,11},{10,... | collective-permute-start | bytes 1572872 | tf_op jit(solution)/shard_map/ppermute | solution.py:389
  62.3 2.0 %cast_shares.6 = (bf16[512,512]{1,0:T(8,128)(2,1)S(1)}, bf16[512,512]{1,0:T(8,128)(2,1)S(1)}, bf16[512,512]{1,0:T(8,128)(2,1)S(1)}) custom-call(f32[2048,2048]{1,0:T(8,128)} %bitcast.20, bf16[512,512]{1,0:T(8,128)(2,1)S(1)} %get-tuple-element.74.refs_0_), custom_call_target="tpu_custom_call" | custom-call | bytes 1024 | tf_op jit(solution)/shard_map/cast_shares/pallas_call | solution.py:81
  64.4 6.4 %update_chunk.5 = (f32[512,2048]{1,0:T(8,128)}, f32[512,2048]{1,0:T(8,128)}, f32[512,2048]{1,0:T(8,128)}, f32[512,128]{1,0:T(8,128)S(1)}, bf16[512,512]{1,0:T(8,128)(2,1)S(1)}) custom-call(s32[1]{0:T(128)} %bitcast.group_ref, f32[2048,2048]{1,0:T(8,128)} %bitcast.21, ...), custom_call_target="tpu_custom_call", output_to_operand_aliasing={{0}: (9, {}), {1}: (10, {}), {2}: (11, {})} | custom-call | bytes 1024 | tf_op jit(solution)/shard_map/update_chunk/pallas_call | solution.py:170
  70.8 3.8 %collective-permute-start.12 = (bf16[512,512]{1,0:T(8,128)(2,1)S(1)}, bf16[512,512]{1,0:T(8,128)(2,1)S(1)}, u32[]{:S(2)}, u32[]{:S(2)}) collective-permute-start(bf16[512,512]{1,0:T(8,128)(2,1)S(1)} %get-tuple-element.84.refs_3_.refs_0_), channel_id=1, source_target_pairs={{0,2},{1,3},{2,6},{3,7},{6,4},{7,5},{4,0},{5,1},{8,10},{9,11},{10,... | collective-permute-start | bytes 1572872 | tf_op jit(solution)/shard_map/ppermute | solution.py:389
  74.7 1.5 collective-permute-start.10
  76.2 1.4 collective-permute-start.11
  78.2 18.5 %collective-permute-done.12.refs_11_.refs_1_ = bf16[512,512]{1,0:T(8,128)(2,1)S(1)} collective-permute-done((bf16[512,512]{1,0:T(8,128)(2,1)S(1)}, bf16[512,512]{1,0:T(8,128)(2,1)S(1)}, u32[]{:S(2)}, u32[]{:S(2)}) %collective-permute-start.12) | collective-permute-done | bytes 524320 | tf_op jit(solution)/shard_map/ppermute | solution.py:389
  96.7 2.0 %cast_shares.7 = (bf16[512,512]{1,0:T(8,128)(2,1)S(1)}, bf16[512,512]{1,0:T(8,128)(2,1)S(1)}, bf16[512,512]{1,0:T(8,128)(2,1)S(1)}) custom-call(f32[2048,2048]{1,0:T(8,128)} %bitcast.22, bf16[512,512]{1,0:T(8,128)(2,1)S(1)} %get-tuple-element.85.refs_0_), custom_call_target="tpu_custom_call" | custom-call | bytes 1024 | tf_op jit(solution)/shard_map/cast_shares/pallas_call | solution.py:81
  98.7 0.8 collective-permute-done.9.refs_0_
  99.5 6.4 %update_chunk.6 = (f32[512,2048]{1,0:T(8,128)}, f32[512,2048]{1,0:T(8,128)}, f32[512,2048]{1,0:T(8,128)}, f32[512,128]{1,0:T(8,128)S(1)}, bf16[512,512]{1,0:T(8,128)(2,1)S(1)}) custom-call(s32[1]{0:T(128)} %bitcast.group_ref, f32[2048,2048]{1,0:T(8,128)} %bitcast.23, ...), custom_call_target="tpu_custom_call", output_to_operand_aliasing={{0}: (9, {}), {1}: (10, {}), {2}: (11, {})} | custom-call | bytes 1024 | tf_op jit(solution)/shard_map/update_chunk/pallas_call | solution.py:170
  105.9 2.2 %collective-permute-done.14.refs_4_.refs_3_ = bf16[512,512]{1,0:T(8,128)(2,1)S(1)} collective-permute-done((bf16[512,512]{1,0:T(8,128)(2,1)S(1)}, bf16[512,512]{1,0:T(8,128)(2,1)S(1)}, u32[]{:S(2)}, u32[]{:S(2)}) %collective-permute-start.14) | collective-permute-done | bytes 524320 | tf_op jit(solution)/shard_map/ppermute | solution.py:389
  108.0 2.1 %collective-permute-start.16 = (bf16[512,512]{1,0:T(8,128)(2,1)S(1)}, bf16[512,512]{1,0:T(8,128)(2,1)S(1)}, u32[]{:S(2)}, u32[]{:S(2)}) collective-permute-start(bf16[512,512]{1,0:T(8,128)(2,1)S(1)} %get-tuple-element.97), channel_id=1, source_target_pairs={{0,16},{8,24},{16,0},{24,8},{1,17},{9,25},{17,1},{25,9},{2,18},{10... | collective-permute-start | bytes 1572872 | tf_op jit(solution)/shard_map/ppermute | solution.py:380
  110.2 1.0 collective-permute-start.17
  111.7 2.9 %collective-permute-start.19 = (bf16[512,512]{1,0:T(8,128)(2,1)S(1)}, bf16[512,512]{1,0:T(8,128)(2,1)S(1)}, u32[]{:S(2)}, u32[]{:S(2)}) collective-permute-start(bf16[512,512]{1,0:T(8,128)(2,1)S(1)} %get-tuple-element.95.refs_3_.refs_0_), channel_id=1, source_target_pairs={{0,4},{1,5},{2,0},{3,1},{6,2},{7,3},{4,6},{5,7},{8,12},{9,13},{10,... | collective-permute-start | bytes 1572872 | tf_op jit(solution)/shard_map/ppermute | solution.py:389
  114.6 2.2 %pick_rows.4 = (bf16[4,256,512]{2,1,0:T(8,128)(2,1)S(1)}, bf16[4,256,512]{2,1,0:T(8,128)(2,1)S(1)}) custom-call(bf16[512,512]{1,0:T(8,128)(2,1)S(1)} %bitcast.11, bf16[512,512]{1,0:T(8,128)(2,1)S(1)} %get-tuple-element.73.refs_3_.refs_0_, bf16[512,512]{1,0:T(8,128)(2,1)S(1)} %collective-permute-done.6.refs_11_.refs_1_, ...), custom_call_target="tpu_custom_call" | custom-call | bytes 1024 | tf_op jit(solution)/shard_map/pick_rows/pallas_call | solution.py:264
  116.8 12.1 %collective-permute-done.16.refs_1_ = bf16[512,512]{1,0:T(8,128)(2,1)S(1)} collective-permute-done((bf16[512,512]{1,0:T(8,128)(2,1)S(1)}, bf16[512,512]{1,0:T(8,128)(2,1)S(1)}, u32[]{:S(2)}, u32[]{:S(2)}) %collective-permute-start.16) | collective-permute-done | bytes 524320 | tf_op jit(solution)/shard_map/ppermute | solution.py:380
  128.9 2.8 %pick_rows.5 = (bf16[4,256,512]{2,1,0:T(8,128)(2,1)S(1)}, bf16[4,256,512]{2,1,0:T(8,128)(2,1)}) custom-call(bf16[512,512]{1,0:T(8,128)(2,1)S(1)} %bitcast.12, bf16[512,512]{1,0:T(8,128)(2,1)S(1)} %get-tuple-element.84.refs_3_.refs_0_, bf16[512,512]{1,0:T(8,128)(2,1)S(1)} %collective-permute-done.12.refs_11_.refs_1_, ...), custom_call_target="tpu_custom_call" | custom-call | bytes 1024 | tf_op jit(solution)/shard_map/pick_rows/pallas_call | solution.py:264
  132.2 1.1 collective-permute-start.20
  133.4 6.3 %update_chunk.7 = (f32[512,2048]{1,0:T(8,128)}, f32[512,2048]{1,0:T(8,128)}, f32[512,2048]{1,0:T(8,128)}, f32[512,128]{1,0:T(8,128)}, bf16[528,512]{1,0:T(8,128)(2,1)S(1)}, /*index=5*/f32[8,512]{1,0:T(8,128)S(1)}) custom-call(s32[1]{0:T(128)} %bitcast.group_ref, f32[2048,2048]{1,0:T(8,128)} %bitcast.24, ...), custom_call_target="tpu_custom_call", output_to_operand_aliasing={{0}: (9, {}), {1}: (10, {}), {2}: (11, {})} | custom-call | bytes 1024 | tf_op jit(solution)/shard_map/update_chunk/pallas_call | solution.py:170
  139.7 1.8 collective-permute-start.23
  141.5 3.1 %collective-permute-start.22 = (bf16[528,512]{1,0:T(8,128)(2,1)S(1)}, bf16[528,512]{1,0:T(8,128)(2,1)S(1)}, u32[]{:S(2)}, u32[]{:S(2)}) collective-permute-start(bf16[528,512]{1,0:T(8,128)(2,1)S(1)} %get-tuple-element.108.refs_1_.refs_0_), channel_id=1, source_target_pairs={{0,2},{1,3},{2,6},{3,7},{6,4},{7,5},{4,0},{5,1},{8,10},{9,11},{10,... | collective-permute-start | bytes 1622024 | tf_op jit(solution)/shard_map/ppermute | solution.py:389
  144.6 3.4 %collective-permute-done.20.refs_2_.refs_3_ = bf16[512,512]{1,0:T(8,128)(2,1)S(1)} collective-permute-done((bf16[512,512]{1,0:T(8,128)(2,1)S(1)}, bf16[512,512]{1,0:T(8,128)(2,1)S(1)}, u32[]{:S(2)}, u32[]{:S(2)}) %collective-permute-start.20) | collective-permute-done | bytes 524320 | tf_op jit(solution)/shard_map/ppermute | solution.py:389
  148.0 16.8 %collective-permute-start.21 = (f32[8,512]{1,0:T(8,128)S(1)}, f32[8,512]{1,0:T(8,128)S(1)}, u32[]{:S(2)}, u32[]{:S(2)}) collective-permute-start(f32[8,512]{1,0:T(8,128)S(1)} %get-tuple-element.109.high_ref), channel_id=1, source_target_pairs={{0,6},{1,7},{2,4},{3,5},{6,0},{7,1},{4,2},{5,3},{8,14},{9,15},{10,... | collective-permute-start | bytes 49160 | tf_op jit(solution)/shard_map/ppermute | solution.py:389
  164.7 2.2 %pick_rows.6 = (bf16[4,256,512]{2,1,0:T(8,128)(2,1)S(1)}, bf16[4,256,512]{2,1,0:T(8,128)(2,1)S(1)}) custom-call(bf16[512,512]{1,0:T(8,128)(2,1)S(1)} %bitcast.13, bf16[512,512]{1,0:T(8,128)(2,1)S(1)} %get-tuple-element.95.refs_3_.refs_0_, bf16[512,512]{1,0:T(8,128)(2,1)S(1)} %pass_after.8.refs_10_.refs_11_.refs_1_, ...), custom_call_target="tpu_custom_call" | custom-call | bytes 16777216 | tf_op jit(solution)/shard_map/pick_rows/pallas_call | solution.py:264
  166.9 6.3 %collective-permute-done.21.across_ref = f32[8,512]{1,0:T(8,128)S(1)} collective-permute-done((f32[8,512]{1,0:T(8,128)S(1)}, f32[8,512]{1,0:T(8,128)S(1)}, u32[]{:S(2)}, u32[]{:S(2)}) %collective-permute-start.21) | collective-permute-done | bytes 16416 | tf_op jit(solution)/shard_map/ppermute | solution.py:389
  173.5 2.8 %collective-permute-start.26 = (bf16[512,256]{1,0:T(8,128)(2,1)S(1)}, bf16[512,256]{1,0:T(8,128)(2,1)S(1)}, u32[]{:S(2)}, u32[]{:S(2)}) collective-permute-start(bf16[512,256]{1,0:T(8,128)(2,1)S(1)} %get-tuple-element.112.refs_3_), channel_id=1, source_target_pairs={{0,4},{1,5},{2,0},{3,1},{6,2},{7,3},{4,6},{5,7},{8,12},{9,13},{10,... | collective-permute-start | bytes 786440 | tf_op jit(solution)/shard_map/ppermute | solution.py:389
  176.3 1.2 collective-permute-done.24.refs_1_
  177.6 0.7 slot_scales.1
  178.4 0.7 copy-done
  179.1 2.4 %store_rows.4 = (bf16[256,16384]{1,0:T(8,128)(2,1)}, f32[8,128]{1,0:T(8,128)S(1)}) custom-call(s32[8]{0:T(128)S(1)} %pass_after.9.refs_4_.place_ref, f32[256,1]{1,0:T(8,128)S(1)} %get-tuple-element.113.inverse_ref, bf16[4,256,512]{2,1,0:T(8,128)(2,1)S(1)} %get-tuple-element.103.refs_4_.mine_ref, bf16[4,256,512]{2,1,0:T(8,128)(2,1)S(1)} %collective-permute-done.28.other_ref, ...), custom_call_target="tpu_custom_call" | custom-call | bytes 1024 | tf_op jit(solution)/shard_map/store_rows/pallas_call | solution.py:298
  181.5 2.4 %store_rows.5 = (bf16[256,16384]{1,0:T(8,128)(2,1)}, f32[8,128]{1,0:T(8,128)S(1)}) custom-call(s32[8]{0:T(128)S(1)} %pass_after.9.refs_4_.place_ref, f32[256,1]{1,0:T(8,128)S(1)} %get-tuple-element.113.inverse_ref, bf16[4,256,512]{2,1,0:T(8,128)(2,1)S(1)} %get-tuple-element.104.refs_1_.mine_ref, ...), custom_call_target="tpu_custom_call", output_to_operand_aliasing={{0}: (4, {})} | custom-call | bytes 1024 | tf_op jit(solution)/shard_map/store_rows/pallas_call | solution.py:298
  183.8 3.5 %collective-permute-done.26.refs_4_ = bf16[512,256]{1,0:T(8,128)(2,1)S(1)} collective-permute-done((bf16[512,256]{1,0:T(8,128)(2,1)S(1)}, bf16[512,256]{1,0:T(8,128)(2,1)S(1)}, u32[]{:S(2)}, u32[]{:S(2)}) %collective-permute-start.26) | collective-permute-done | bytes 262176 | tf_op jit(solution)/shard_map/ppermute | solution.py:389
  187.4 2.2 %pick_rows.7 = (bf16[4,256,512]{2,1,0:T(8,128)(2,1)S(1)}, bf16[4,256,512]{2,1,0:T(8,128)(2,1)S(1)}) custom-call(bf16[512,512]{1,0:T(8,128)(2,1)S(1)} %bitcast.15, bf16[528,512]{1,0:T(8,128)(2,1)S(1)} %get-tuple-element.108.refs_1_.refs_0_, bf16[528,512]{1,0:T(8,128)(2,1)S(1)} %collective-permute-done.22.ahead_ref.refs_1_, ...), custom_call_target="tpu_custom_call" | custom-call | bytes 1024 | tf_op jit(solution)/shard_map/pick_rows/pallas_call | solution.py:264
  189.6 2.4 %store_rows.6 = (bf16[256,16384]{1,0:T(8,128)(2,1)}, f32[8,128]{1,0:T(8,128)S(1)}) custom-call(s32[8]{0:T(128)S(1)} %pass_after.9.refs_4_.place_ref, f32[256,1]{1,0:T(8,128)S(1)} %get-tuple-element.113.inverse_ref, bf16[4,256,512]{2,1,0:T(8,128)(2,1)S(1)} %get-tuple-element.110.refs_0_.mine_ref, ...), custom_call_target="tpu_custom_call", output_to_operand_aliasing={{0}: (4, {})} | custom-call | bytes 1024 | tf_op jit(solution)/shard_map/store_rows/pallas_call | solution.py:298
  192.3 3.0 %store_rows.7 = (bf16[256,16384]{1,0:T(8,128)(2,1)}, f32[8,128]{1,0:T(8,128)}) custom-call(s32[8]{0:T(128)S(1)} %pass_after.9.refs_4_.place_ref, f32[256,1]{1,0:T(8,128)S(1)} %get-tuple-element.113.inverse_ref, bf16[4,256,512]{2,1,0:T(8,128)(2,1)S(1)} %get-tuple-element.120.refs_1_.mine_ref, ...), custom_call_target="tpu_custom_call", output_to_operand_aliasing={{0}: (4, {})} | custom-call | bytes 1024 | tf_op jit(solution)/shard_map/store_rows/pallas_call | solution.py:298
  (60 shorter events, 5.2 us)
Async XLA Ops:
  0.6 6.7 %copy-start.1 = (s32[4]{0:T(128)S(1)}, s32[4]{0:T(128)}, u32[]{:S(2)}) copy-start(s32[4]{0:T(128)} %constant.62.clone) | copy-start | bytes 52
  0.6 7.3 %copy-start.4 = (s32[4]{0:T(128)S(1)}, s32[4]{0:T(128)}, u32[]{:S(2)}) copy-start(s32[4]{0:T(128)} %constant.63.clone) | copy-start | bytes 52
  0.7 8.7 %copy-start.3 = (s32[512]{0:T(512)S(1)}, s32[512]{0:T(512)}, u32[]{:S(2)}) copy-start(s32[512]{0:T(512)} %param.13) | copy-start | bytes 6148
  0.7 8.9 %copy-start.2 = (s32[512]{0:T(512)S(1)}, s32[512]{0:T(512)}, u32[]{:S(2)}) copy-start(s32[512]{0:T(512)} %param.14) | copy-start | bytes 6148
  2.7 26.2 %collective-permute-start.1 = (bf16[512,512]{1,0:T(8,128)(2,1)S(1)}, bf16[512,512]{1,0:T(8,128)(2,1)S(1)}, u32[]{:S(2)}, u32[]{:S(2)}) collective-permute-start(bf16[512,512]{1,0:T(8,128)(2,1)S(1)} %get-tuple-element.71), channel_id=1, source_target_pairs={{0,16},{8,24},{16,0},{24,8},{1,17},{9,25},{17,1},{25,9},{2,18},{10... | collective-permute-start | bytes 1572872 | tf_op jit(solution)/shard_map/ppermute | solution.py:380
  5.7 23.2 %collective-permute-start.2 = (bf16[512,512]{1,0:T(8,128)(2,1)S(1)}, bf16[512,512]{1,0:T(8,128)(2,1)S(1)}, u32[]{:S(2)}, u32[]{:S(2)}) collective-permute-start(bf16[512,512]{1,0:T(8,128)(2,1)S(1)} %get-tuple-element.72), channel_id=1, source_target_pairs={{0,24},{8,16},{16,8},{24,0},{1,25},{9,17},{17,9},{25,1},{2,26},{10... | collective-permute-start | bytes 1572872 | tf_op jit(solution)/shard_map/ppermute | solution.py:380
  7.2 23.0 %collective-permute-start = (bf16[512,512]{1,0:T(8,128)(2,1)S(1)}, bf16[512,512]{1,0:T(8,128)(2,1)S(1)}, u32[]{:S(2)}, u32[]{:S(2)}) collective-permute-start(bf16[512,512]{1,0:T(8,128)(2,1)S(1)} %get-tuple-element.66.refs_0_), channel_id=1, source_target_pairs={{0,8},{8,0},{16,24},{24,16},{1,9},{9,1},{17,25},{25,17},{2,10},{10... | collective-permute-start | bytes 1572872 | tf_op jit(solution)/shard_map/ppermute | solution.py:380
  36.3 15.3 %collective-permute-start.6 = (bf16[512,512]{1,0:T(8,128)(2,1)S(1)}, bf16[512,512]{1,0:T(8,128)(2,1)S(1)}, u32[]{:S(2)}, u32[]{:S(2)}) collective-permute-start(bf16[512,512]{1,0:T(8,128)(2,1)S(1)} %get-tuple-element.73.refs_3_.refs_0_), channel_id=1, source_target_pairs={{0,2},{1,3},{2,6},{3,7},{6,4},{7,5},{4,0},{5,1},{8,10},{9,11},{10,... | collective-permute-start | bytes 1572872 | tf_op jit(solution)/shard_map/ppermute | solution.py:389
  38.1 26.2 %collective-permute-start.4 = (bf16[512,512]{1,0:T(8,128)(2,1)S(1)}, bf16[512,512]{1,0:T(8,128)(2,1)S(1)}, u32[]{:S(2)}, u32[]{:S(2)}) collective-permute-start(bf16[512,512]{1,0:T(8,128)(2,1)S(1)} %get-tuple-element.78), channel_id=1, source_target_pairs={{0,16},{8,24},{16,0},{24,8},{1,17},{9,25},{17,1},{25,9},{2,18},{10... | collective-permute-start | bytes 1572872 | tf_op jit(solution)/shard_map/ppermute | solution.py:380
  39.6 24.7 %collective-permute-start.5 = (bf16[512,512]{1,0:T(8,128)(2,1)S(1)}, bf16[512,512]{1,0:T(8,128)(2,1)S(1)}, u32[]{:S(2)}, u32[]{:S(2)}) collective-permute-start(bf16[512,512]{1,0:T(8,128)(2,1)S(1)} %get-tuple-element.79), channel_id=1, source_target_pairs={{0,24},{8,16},{16,8},{24,0},{1,25},{9,17},{17,9},{25,1},{2,26},{10... | collective-permute-start | bytes 1572872 | tf_op jit(solution)/shard_map/ppermute | solution.py:380
  41.0 23.3 %collective-permute-start.3 = (bf16[512,512]{1,0:T(8,128)(2,1)S(1)}, bf16[512,512]{1,0:T(8,128)(2,1)S(1)}, u32[]{:S(2)}, u32[]{:S(2)}) collective-permute-start(bf16[512,512]{1,0:T(8,128)(2,1)S(1)} %get-tuple-element.74.refs_0_), channel_id=1, source_target_pairs={{0,8},{8,0},{16,24},{24,16},{1,9},{9,1},{17,25},{25,17},{2,10},{10... | collective-permute-start | bytes 1572872 | tf_op jit(solution)/shard_map/ppermute | solution.py:380
  41.5 22.9 %collective-permute-start.7 = (bf16[512,512]{1,0:T(8,128)(2,1)S(1)}, bf16[512,512]{1,0:T(8,128)(2,1)S(1)}, u32[]{:S(2)}, u32[]{:S(2)}) collective-permute-start(bf16[512,512]{1,0:T(8,128)(2,1)S(1)} %get-tuple-element.73.refs_3_.refs_0_), channel_id=1, source_target_pairs={{0,4},{1,5},{2,0},{3,1},{6,2},{7,3},{4,6},{5,7},{8,12},{9,13},{10,... | collective-permute-start | bytes 1572872 | tf_op jit(solution)/shard_map/ppermute | solution.py:389
  51.5 23.1 %collective-permute-start.8 = (bf16[512,512]{1,0:T(8,128)(2,1)S(1)}, bf16[512,512]{1,0:T(8,128)(2,1)S(1)}, u32[]{:S(2)}, u32[]{:S(2)}) collective-permute-start(bf16[512,512]{1,0:T(8,128)(2,1)S(1)} %collective-permute-done.6.refs_11_.refs_1_), channel_id=1, source_target_pairs={{0,2},{1,3},{2,6},{3,7},{6,4},{7,5},{4,0},{5,1},{8,10},{9,11},{10,... | collective-permute-start | bytes 1572872 | tf_op jit(solution)/shard_map/ppermute | solution.py:389
  70.8 25.8 %collective-permute-start.12 = (bf16[512,512]{1,0:T(8,128)(2,1)S(1)}, bf16[512,512]{1,0:T(8,128)(2,1)S(1)}, u32[]{:S(2)}, u32[]{:S(2)}) collective-permute-start(bf16[512,512]{1,0:T(8,128)(2,1)S(1)} %get-tuple-element.84.refs_3_.refs_0_), channel_id=1, source_target_pairs={{0,2},{1,3},{2,6},{3,7},{6,4},{7,5},{4,0},{5,1},{8,10},{9,11},{10,... | collective-permute-start | bytes 1572872 | tf_op jit(solution)/shard_map/ppermute | solution.py:389
  74.7 24.0 %collective-permute-start.13 = (bf16[512,512]{1,0:T(8,128)(2,1)S(1)}, bf16[512,512]{1,0:T(8,128)(2,1)S(1)}, u32[]{:S(2)}, u32[]{:S(2)}) collective-permute-start(bf16[512,512]{1,0:T(8,128)(2,1)S(1)} %get-tuple-element.84.refs_3_.refs_0_), channel_id=1, source_target_pairs={{0,4},{1,5},{2,0},{3,1},{6,2},{7,3},{4,6},{5,7},{8,12},{9,13},{10,... | collective-permute-start | bytes 1572872 | tf_op jit(solution)/shard_map/ppermute | solution.py:389
  74.7 24.0 %collective-permute-start.10 = (bf16[512,512]{1,0:T(8,128)(2,1)S(1)}, bf16[512,512]{1,0:T(8,128)(2,1)S(1)}, u32[]{:S(2)}, u32[]{:S(2)}) collective-permute-start(bf16[512,512]{1,0:T(8,128)(2,1)S(1)} %get-tuple-element.89), channel_id=1, source_target_pairs={{0,16},{8,24},{16,0},{24,8},{1,17},{9,25},{17,1},{25,9},{2,18},{10... | collective-permute-start | bytes 1572872 | tf_op jit(solution)/shard_map/ppermute | solution.py:380
  76.2 22.5 %collective-permute-start.11 = (bf16[512,512]{1,0:T(8,128)(2,1)S(1)}, bf16[512,512]{1,0:T(8,128)(2,1)S(1)}, u32[]{:S(2)}, u32[]{:S(2)}) collective-permute-start(bf16[512,512]{1,0:T(8,128)(2,1)S(1)} %get-tuple-element.90), channel_id=1, source_target_pairs={{0,24},{8,16},{16,8},{24,0},{1,25},{9,17},{17,9},{25,1},{2,26},{10... | collective-permute-start | bytes 1572872 | tf_op jit(solution)/shard_map/ppermute | solution.py:380
  77.6 21.8 %collective-permute-start.9 = (bf16[512,512]{1,0:T(8,128)(2,1)S(1)}, bf16[512,512]{1,0:T(8,128)(2,1)S(1)}, u32[]{:S(2)}, u32[]{:S(2)}) collective-permute-start(bf16[512,512]{1,0:T(8,128)(2,1)S(1)} %get-tuple-element.85.refs_0_), channel_id=1, source_target_pairs={{0,8},{8,0},{16,24},{24,16},{1,9},{9,1},{17,25},{25,17},{2,10},{10... | collective-permute-start | bytes 1572872 | tf_op jit(solution)/shard_map/ppermute | solution.py:380
  96.7 11.4 %collective-permute-start.14 = (bf16[512,512]{1,0:T(8,128)(2,1)S(1)}, bf16[512,512]{1,0:T(8,128)(2,1)S(1)}, u32[]{:S(2)}, u32[]{:S(2)}) collective-permute-start(bf16[512,512]{1,0:T(8,128)(2,1)S(1)} %collective-permute-done.12.refs_11_.refs_1_), channel_id=1, source_target_pairs={{0,2},{1,3},{2,6},{3,7},{6,4},{7,5},{4,0},{5,1},{8,10},{9,11},{10,... | collective-permute-start | bytes 1572872 | tf_op jit(solution)/shard_map/ppermute | solution.py:389
  108.0 20.8 %collective-permute-start.16 = (bf16[512,512]{1,0:T(8,128)(2,1)S(1)}, bf16[512,512]{1,0:T(8,128)(2,1)S(1)}, u32[]{:S(2)}, u32[]{:S(2)}) collective-permute-start(bf16[512,512]{1,0:T(8,128)(2,1)S(1)} %get-tuple-element.97), channel_id=1, source_target_pairs={{0,16},{8,24},{16,0},{24,8},{1,17},{9,25},{17,1},{25,9},{2,18},{10... | collective-permute-start | bytes 1572872 | tf_op jit(solution)/shard_map/ppermute | solution.py:380
  110.2 21.4 %collective-permute-start.18 = (bf16[512,512]{1,0:T(8,128)(2,1)S(1)}, bf16[512,512]{1,0:T(8,128)(2,1)S(1)}, u32[]{:S(2)}, u32[]{:S(2)}) collective-permute-start(bf16[512,512]{1,0:T(8,128)(2,1)S(1)} %get-tuple-element.95.refs_3_.refs_0_), channel_id=1, source_target_pairs={{0,2},{1,3},{2,6},{3,7},{6,4},{7,5},{4,0},{5,1},{8,10},{9,11},{10,... | collective-permute-start | bytes 1572872 | tf_op jit(solution)/shard_map/ppermute | solution.py:389
  110.2 22.0 %collective-permute-start.17 = (bf16[512,512]{1,0:T(8,128)(2,1)S(1)}, bf16[512,512]{1,0:T(8,128)(2,1)S(1)}, u32[]{:S(2)}, u32[]{:S(2)}) collective-permute-start(bf16[512,512]{1,0:T(8,128)(2,1)S(1)} %get-tuple-element.98), channel_id=1, source_target_pairs={{0,24},{8,16},{16,8},{24,0},{1,25},{9,17},{17,9},{25,1},{2,26},{10... | collective-permute-start | bytes 1572872 | tf_op jit(solution)/shard_map/ppermute | solution.py:380
  111.2 22.2 %collective-permute-start.15 = (bf16[512,512]{1,0:T(8,128)(2,1)S(1)}, bf16[512,512]{1,0:T(8,128)(2,1)S(1)}, u32[]{:S(2)}, u32[]{:S(2)}) collective-permute-start(bf16[512,512]{1,0:T(8,128)(2,1)S(1)} %get-tuple-element.96.refs_4_), channel_id=1, source_target_pairs={{0,8},{8,0},{16,24},{24,16},{1,9},{9,1},{17,25},{25,17},{2,10},{10... | collective-permute-start | bytes 1572872 | tf_op jit(solution)/shard_map/ppermute | solution.py:380
  111.7 21.6 %collective-permute-start.19 = (bf16[512,512]{1,0:T(8,128)(2,1)S(1)}, bf16[512,512]{1,0:T(8,128)(2,1)S(1)}, u32[]{:S(2)}, u32[]{:S(2)}) collective-permute-start(bf16[512,512]{1,0:T(8,128)(2,1)S(1)} %get-tuple-element.95.refs_3_.refs_0_), channel_id=1, source_target_pairs={{0,4},{1,5},{2,0},{3,1},{6,2},{7,3},{4,6},{5,7},{8,12},{9,13},{10,... | collective-permute-start | bytes 1572872 | tf_op jit(solution)/shard_map/ppermute | solution.py:389
  128.8 49.5 %collective-permute-start.28 = (bf16[4,256,512]{2,1,0:T(8,128)(2,1)S(1)}, bf16[4,256,512]{2,1,0:T(8,128)(2,1)S(1)}, u32[]{:S(2)}, u32[]{:S(2)}) collective-permute-start(bf16[4,256,512]{2,1,0:T(8,128)(2,1)S(1)} %get-tuple-element.115), channel_id=1, source_target_pairs={{0,1},{1,0},{2,3},{3,2},{4,5},{5,4},{6,7},{7,6},{8,9},{9,8},{10,11... | collective-permute-start | bytes 3145736 | tf_op jit(solution)/shard_map/ppermute | solution.py:392
  131.6 49.8 %collective-permute-start.27 = (bf16[4,256,512]{2,1,0:T(8,128)(2,1)}, bf16[4,256,512]{2,1,0:T(8,128)(2,1)S(1)}, u32[]{:S(2)}, u32[]{:S(2)}) collective-permute-start(bf16[4,256,512]{2,1,0:T(8,128)(2,1)} %get-tuple-element.114), channel_id=1, source_target_pairs={{0,1},{1,0},{2,3},{3,2},{4,5},{5,4},{6,7},{7,6},{8,9},{9,8},{10,11... | collective-permute-start | bytes 3145736 | tf_op jit(solution)/shard_map/ppermute | solution.py:392
  132.2 15.8 %collective-permute-start.20 = (bf16[512,512]{1,0:T(8,128)(2,1)S(1)}, bf16[512,512]{1,0:T(8,128)(2,1)S(1)}, u32[]{:S(2)}, u32[]{:S(2)}) collective-permute-start(bf16[512,512]{1,0:T(8,128)(2,1)S(1)} %pass_after.8.refs_10_.refs_11_.refs_1_), channel_id=1, source_target_pairs={{0,2},{1,3},{2,6},{3,7},{6,4},{7,5},{4,0},{5,1},{8,10},{9,11},{10,... | collective-permute-start | bytes 1572872 | tf_op jit(solution)/shard_map/ppermute | solution.py:389
  139.7 33.5 %collective-permute-start.23 = (bf16[528,512]{1,0:T(8,128)(2,1)S(1)}, bf16[528,512]{1,0:T(8,128)(2,1)S(1)}, u32[]{:S(2)}, u32[]{:S(2)}) collective-permute-start(bf16[528,512]{1,0:T(8,128)(2,1)S(1)} %get-tuple-element.108.refs_1_.refs_0_), channel_id=1, source_target_pairs={{0,4},{1,5},{2,0},{3,1},{6,2},{7,3},{4,6},{5,7},{8,12},{9,13},{10,... | collective-permute-start | bytes 1622024 | tf_op jit(solution)/shard_map/ppermute | solution.py:389
  141.5 31.7 %collective-permute-start.22 = (bf16[528,512]{1,0:T(8,128)(2,1)S(1)}, bf16[528,512]{1,0:T(8,128)(2,1)S(1)}, u32[]{:S(2)}, u32[]{:S(2)}) collective-permute-start(bf16[528,512]{1,0:T(8,128)(2,1)S(1)} %get-tuple-element.108.refs_1_.refs_0_), channel_id=1, source_target_pairs={{0,2},{1,3},{2,6},{3,7},{6,4},{7,5},{4,0},{5,1},{8,10},{9,11},{10,... | collective-permute-start | bytes 1622024 | tf_op jit(solution)/shard_map/ppermute | solution.py:389
  148.0 25.2 %collective-permute-start.21 = (f32[8,512]{1,0:T(8,128)S(1)}, f32[8,512]{1,0:T(8,128)S(1)}, u32[]{:S(2)}, u32[]{:S(2)}) collective-permute-start(f32[8,512]{1,0:T(8,128)S(1)} %get-tuple-element.109.high_ref), channel_id=1, source_target_pairs={{0,6},{1,7},{2,4},{3,5},{6,0},{7,1},{4,2},{5,3},{8,14},{9,15},{10,... | collective-permute-start | bytes 49160 | tf_op jit(solution)/shard_map/ppermute | solution.py:389
  173.3 10.5 %collective-permute-start.25 = (bf16[512,256]{1,0:T(8,128)(2,1)S(1)}, bf16[512,256]{1,0:T(8,128)(2,1)S(1)}, u32[]{:S(2)}, u32[]{:S(2)}) collective-permute-start(bf16[512,256]{1,0:T(8,128)(2,1)S(1)} %get-tuple-element.111.refs_2_), channel_id=1, source_target_pairs={{0,2},{1,3},{2,6},{3,7},{6,4},{7,5},{4,0},{5,1},{8,10},{9,11},{10,... | collective-permute-start | bytes 786440 | tf_op jit(solution)/shard_map/ppermute | solution.py:389
  173.5 13.8 %collective-permute-start.26 = (bf16[512,256]{1,0:T(8,128)(2,1)S(1)}, bf16[512,256]{1,0:T(8,128)(2,1)S(1)}, u32[]{:S(2)}, u32[]{:S(2)}) collective-permute-start(bf16[512,256]{1,0:T(8,128)(2,1)S(1)} %get-tuple-element.112.refs_3_), channel_id=1, source_target_pairs={{0,4},{1,5},{2,0},{3,1},{6,2},{7,3},{4,6},{5,7},{8,12},{9,13},{10,... | collective-permute-start | bytes 786440 | tf_op jit(solution)/shard_map/ppermute | solution.py:389
  176.3 1.2 collective-permute-start.24
  177.5 12.2 %collective-permute-start.30 = (bf16[4,256,512]{2,1,0:T(8,128)(2,1)S(1)}, bf16[4,256,512]{2,1,0:T(8,128)(2,1)S(1)}, u32[]{:S(2)}, u32[]{:S(2)}) collective-permute-start(bf16[4,256,512]{2,1,0:T(8,128)(2,1)S(1)} %get-tuple-element.122), channel_id=1, source_target_pairs={{0,1},{1,0},{2,3},{3,2},{4,5},{5,4},{6,7},{7,6},{8,9},{9,8},{10,11... | collective-permute-start | bytes 3145736 | tf_op jit(solution)/shard_map/ppermute | solution.py:392
  178.4 0.7 copy-start
  189.5 2.7 %collective-permute-start.29 = (bf16[4,256,512]{2,1,0:T(8,128)(2,1)S(1)}, bf16[4,256,512]{2,1,0:T(8,128)(2,1)S(1)}, u32[]{:S(2)}, u32[]{:S(2)}) collective-permute-start(bf16[4,256,512]{2,1,0:T(8,128)(2,1)S(1)} %get-tuple-element.121), channel_id=1, source_target_pairs={{0,1},{1,0},{2,3},{3,2},{4,5},{5,4},{6,7},{7,6},{8,9},{9,8},{10,11... | collective-permute-start | bytes 3145736 | tf_op jit(solution)/shard_map/ppermute | solution.py:392
